TPU v7x, 32 devices: a whole 2x2x4 slice. The times are simulated.
32 devices in a mesh: seg: 8 (over y, x, core), tok: 4 (over z).
Axes of the slice: x: 2, y: 2, z: 4, core: 2. Of those that a mesh axis runs over, the one named last changes fastest.
Arguments:
- value: bfloat16 [524288, 128], P(('seg', 'tok')), may hold values from -6 to 6
- gate_in: bfloat16 [524288, 128], P(('seg', 'tok')), may hold values from -6 to 6
- gate_out: bfloat16 [524288, 128], P(('seg', 'tok')), may hold values from -6 to 6
- filter_spectrum: bfloat16 [2, 256, 512, 128], P(None, 'tok'), may hold values from -8 to 8, as said below
- skip_gain: float32 [128], replicated, may hold values from 0.25 to 2
Outputs:
- mixed_out: bfloat16 [524288, 128], P(('seg', 'tok'))
Inputs may be any that keep to these rules, and one draw needn't show every extreme that they name: `filter_spectrum`: the response of a real filter whose taps beyond the first 65536 are zero, rounded.
All inputs are finite; a program needn't handle non-finite values.
Results may differ from a plain program's by a relative error of at most 0.0085.
Values may be sent and summed in bfloat16 or wider, within the bound.
A program may use at most 192 MiB of HBM per device.

v0:
```python
import math

import jax
import jax.numpy as jnp
from jax import lax
from jax.sharding import PartitionSpec as P

N1 = 256
N2 = 512


def passed_along(value, axis, by):
    devices = lax.axis_size(axis)
    pairs = [(i, i + by) for i in range(devices) if 0 <= i + by < devices]
    return lax.ppermute(value, axis, pairs)


def span_ids(count):
    return jnp.arange(count, dtype=jnp.int32)


def trig_tables(row_ids, col_ids, modulus):
    product = row_ids[:, None] * col_ids[None, :] % modulus
    angle = product.astype(jnp.float32) * jnp.float32(2.0 * math.pi / modulus)
    return (jnp.cos(angle), jnp.sin(angle))


def einsum_lanes(data, table):
    return jnp.einsum("ckn,nm->ckm", data, table, preferred_element_type=jnp.float32)


def channel_transform(data, spectrum, tables, tw_cos, tw_sin, scale):
    cos_one, nsin_one, cos_two, sin_two, inv_cos, inv_nsin = tables
    a_real = jnp.einsum("kj,cjn->ckn", cos_one, data, preferred_element_type=jnp.float32)
    a_imag = jnp.einsum("kj,cjn->ckn", nsin_one, data, preferred_element_type=jnp.float32)
    t_cos = tw_cos[None]
    t_sin = tw_sin[None]
    b_real = (a_real * t_cos + a_imag * t_sin).astype(jnp.bfloat16)
    b_imag = (a_imag * t_cos - a_real * t_sin).astype(jnp.bfloat16)
    x_real = einsum_lanes(b_real, cos_two) + einsum_lanes(b_imag, sin_two)
    x_imag = einsum_lanes(b_imag, cos_two) - einsum_lanes(b_real, sin_two)
    h_real = spectrum[0].astype(jnp.float32)
    h_imag = spectrum[1].astype(jnp.float32)
    z_real = (x_real * h_real - x_imag * h_imag).astype(jnp.bfloat16)
    z_imag = (x_real * h_imag + x_imag * h_real).astype(jnp.bfloat16)
    p_real = einsum_lanes(z_real, cos_two) - einsum_lanes(z_imag, sin_two)
    p_imag = einsum_lanes(z_imag, cos_two) + einsum_lanes(z_real, sin_two)
    q_real = (p_real * t_cos - p_imag * t_sin).astype(jnp.bfloat16)
    q_imag = (p_imag * t_cos + p_real * t_sin).astype(jnp.bfloat16)
    total = jnp.einsum("nk,ckm->cnm", inv_cos, q_real, preferred_element_type=jnp.float32)
    total = total + jnp.einsum("nk,ckm->cnm", inv_nsin, q_imag, preferred_element_type=jnp.float32)
    return (total * scale).astype(jnp.bfloat16)


def add_round(first, second):
    return (first.astype(jnp.float32) + second.astype(jnp.float32)).astype(jnp.bfloat16)


def shards(value, gate_in, gate_out, filter_spectrum, skip_gain):
    tok_count = lax.axis_size("tok")
    gated = (value.astype(jnp.float32) * gate_in.astype(jnp.float32)).astype(jnp.bfloat16)
    channels = gated.shape[1]
    fft_len = N1 * N2
    half_rows = N1 // 2
    scale = jnp.float32(1.0 / fft_len)
    cos_one, sin_one = trig_tables(span_ids(N1), span_ids(half_rows), N1)
    cos_one_b = cos_one.astype(jnp.bfloat16)
    nsin_one_b = (-sin_one).astype(jnp.bfloat16)
    cos_two, sin_two = trig_tables(span_ids(N2), span_ids(N2), N2)
    cos_two_b = cos_two.astype(jnp.bfloat16)
    sin_two_b = sin_two.astype(jnp.bfloat16)
    inv_cos, inv_sin = trig_tables(span_ids(N1), span_ids(N1), N1)
    inv_cos_b = inv_cos.astype(jnp.bfloat16)
    inv_nsin_b = (-inv_sin).astype(jnp.bfloat16)
    narrow = channels // tok_count
    whole = lax.all_to_all(gated.T, "tok", split_axis=0, concat_axis=1, tiled=True)
    spectrum = lax.all_to_all(
        jnp.transpose(filter_spectrum, (0, 3, 1, 2)), "tok", split_axis=1, concat_axis=2, tiled=True
    )
    tw_cos, tw_sin = trig_tables(span_ids(N1), span_ids(N2), fft_len)
    tables = (cos_one_b, nsin_one_b, cos_two_b, sin_two_b, inv_cos_b, inv_nsin_b)
    conv = channel_transform(
        whole.reshape(narrow, half_rows, N2), spectrum, tables, tw_cos, tw_sin, scale
    )
    grouped = jnp.transpose(conv.reshape(narrow, 2, tok_count, -1), (1, 2, 0, 3))
    grouped = grouped.reshape(2, tok_count, 1, narrow, -1)
    pieces = lax.all_to_all(grouped, "tok", split_axis=1, concat_axis=3, tiled=True)
    pieces = pieces.reshape(2, channels, -1)
    carried = passed_along(pieces[1], "seg", 1)
    mixed = add_round(pieces[0], carried)
    mixed = mixed.T
    result = gate_out.astype(jnp.float32) * (
        mixed.astype(jnp.float32) + skip_gain[None, :] * gated.astype(jnp.float32)
    )
    return result.astype(jnp.bfloat16)


def solution(mesh):
    return jax.shard_map(
        shards,
        mesh=mesh,
        in_specs=(
            P(("seg", "tok"), None),
            P(("seg", "tok"), None),
            P(("seg", "tok"), None),
            P(None, "tok", None, None),
            P(),
        ),
        out_specs=P(("seg", "tok"), None),
        check_vma=False,
    )
```

profile of v0, /device:TPU:2, one launch (start us, length us, event | category | flops | bytes accessed | tf_op | source)
XLA Modules:
  0.0 977.2 jit_solution(10849499232449880804)
XLA Ops:
  0.0 6.4 copy.37
  12.8 6.5 multiply_convert_fusion.1
  24.1 23.0 %copy.44 = bf16[2,64,512,128]{2,1,0,3:T(8,128)(2,1)} copy(bf16[2,64,512,128]{3,2,1,0:T(8,128)(2,1)} %param.8) | data formatting | bytes 33554432 | tf_op args[3]
  47.1 70.5 %all-to-all-done = bf16[4,32,16384]{2,1,0:T(8,128)(2,1)} async-done(((bf16[4,32,16384]{2,1,0:T(8,128)(2,1)}), bf16[4,32,16384]{2,1,0:T(8,128)(2,1)}, u32[]{:S(2)}, u32[]{:S(2)}) %all-to-all-start) | async-done | bytes 4194336 | tf_op jit(solution)/shard_map/all_to_all | solution.py:76
  117.6 7.5 all-to-all-start.1
  127.2 7.4 copy.39
  134.6 7.7 reshape.71
  142.3 10.9 %fusion.60 = f32[32,512,256]{2,1,0:T(8,128)} fusion(bf16[32,128,512]{2,1,0:T(8,128)(2,1)} %reshape.71), kind=kOutput, calls=%fused_computation.84 | convolution fusion | flops 1074233344 | bytes 20971520 | tf_op jit(solution)/shard_map/kj,cjn->ckn/dot_general | solution.py:34
  153.2 12.7 %fusion.1 = (bf16[32,256,512]{1,2,0:T(8,128)(2,1)}, bf16[32,256,512]{1,2,0:T(8,128)(2,1)}) fusion(f32[32,512,256]{2,1,0:T(8,128)} %fusion.60, f32[256,512]{0,1:T(8,128)S(1)} %get-tuple-element.13, f32[256,512]{0,1:T(8,128)S(1)} %get-tuple-element.14, bf16[32,128,512]{2,1,0:T(8,128)(2,1)S(1)} %copy-done.2), kind=kOutput, calls=%fused_computation.3 | convolution fusion | flops 1107820544 | bytes 38797312 | tf_op jit(solution)/shard_map/kj,cjn->ckn/dot_general | solution.py:35
  165.9 15.5 %fusion.34 = f32[32,256,512]{2,1,0:T(8,128)} fusion(bf16[32,256,512]{1,2,0:T(8,128)(2,1)} %get-tuple-element.7), kind=kOutput, calls=%fused_computation.53 | convolution fusion | flops 4298899456 | bytes 25165824 | tf_op jit(solution)/shard_map/ckn,nm->ckm/dot_general | solution.py:29
  181.4 11.8 %fusion.32 = f32[32,256,512]{2,1,0:T(8,128)} fusion(bf16[32,256,512]{1,2,0:T(8,128)(2,1)S(1)} %copy-done), kind=kOutput, calls=%fused_computation.52 | convolution fusion | flops 4298899456 | bytes 25165824 | tf_op jit(solution)/shard_map/ckn,nm->ckm/dot_general | solution.py:29
  193.2 15.5 %convolution_add_fusion.1 = f32[32,256,512]{2,1,0:T(8,128)} fusion(f32[32,256,512]{2,1,0:T(8,128)} %fusion.34, bf16[32,256,512]{1,2,0:T(8,128)(2,1)S(1)} %copy-done), kind=kOutput, calls=%fused_computation.16 | convolution fusion | flops 4303093760 | bytes 41943040 | tf_op jit(solution)/shard_map/ckn,nm->ckm/dot_general | solution.py:29
  208.7 278.7 %all-to-all-done.1 = bf16[2,128,64,512]{3,2,0,1:T(8,128)(2,1)} async-done(((bf16[2,128,64,512]{3,2,0,1:T(8,128)(2,1)}), bf16[2,128,64,512]{3,2,0,1:T(8,128)(2,1)}, u32[]{:S(2)}, u32[]{:S(2)}) %all-to-all-start.1) | async-done | bytes 16777248 | tf_op jit(solution)/shard_map/all_to_all | solution.py:77
  487.4 14.0 %copy.45 = bf16[2,128,64,512]{3,2,1,0:T(8,128)(2,1)} copy(bf16[2,128,64,512]{3,2,0,1:T(8,128)(2,1)} %all-to-all-done.1) | data formatting | bytes 33554432 | tf_op jit(solution)/shard_map/all_to_all | solution.py:77
  501.4 12.2 %slice_convert_fusion = (f32[1,32,4,64,512]{4,3,1,2,0:T(8,128)S(1)}, f32[1,32,4,64,512]{4,3,1,2,0:T(8,128)}) fusion(bf16[2,32,4,64,512]{4,3,1,2,0:T(8,128)(2,1)} %bitcast.81), kind=kLoop, calls=%fused_computation.18 | loop fusion | flops 8388608 | bytes 50331648 | tf_op jit(solution)/shard_map/convert_element_type | solution.py:43
  513.6 12.0 %copy.46 = f32[1,32,4,64,512]{4,3,2,1,0:T(8,128)} copy(f32[1,32,4,64,512]{4,3,1,2,0:T(8,128)} %get-tuple-element.10) | data formatting | bytes 33554432 | tf_op jit(solution)/shard_map/convert_element_type | solution.py:42
  531.8 34.7 %subtract_convert_fusion.1 = (bf16[32,256,512]{2,1,0:T(8,128)(2,1)}, bf16[32,256,512]{2,1,0:T(8,128)(2,1)}) fusion(f32[32,256,512]{2,1,0:T(8,128)} %bitcast.84, f32[32,256,512]{2,1,0:T(8,128)} %convolution_add_fusion.1, f32[32,256,512]{2,1,0:T(8,128)} %bitcast.83, f32[32,256,512]{2,1,0:T(8,128)} %fusion.32, bf16[32,256,512]{1,2,0:T(8,128)(2,1)} %get-tuple-element.7), kind=kOutput, calls=%fused_computation.12 | convolution fusion | flops 4336648192 | bytes 92274688 | tf_op jit(solution)/shard_map/ckn,nm->ckm/dot_general | solution.py:29
  566.5 15.4 %fusion.30 = f32[32,256,512]{1,2,0:T(8,128)} fusion(bf16[32,256,512]{2,1,0:T(8,128)(2,1)} %get-tuple-element.5), kind=kOutput, calls=%fused_computation.51 | convolution fusion | flops 4298899456 | bytes 25165824 | tf_op jit(solution)/shard_map/ckn,nm->ckm/dot_general | solution.py:29
  582.0 11.5 %fusion.28 = f32[32,256,512]{1,2,0:T(8,128)} fusion(bf16[32,256,512]{2,1,0:T(8,128)(2,1)S(1)} %copy-done.1), kind=kOutput, calls=%fused_computation.50 | convolution fusion | flops 4298899456 | bytes 25165824 | tf_op jit(solution)/shard_map/ckn,nm->ckm/dot_general | solution.py:29
  593.5 17.5 %convolution_subtract_fusion = f32[32,256,512]{1,2,0:T(8,128)} fusion(f32[32,256,512]{1,2,0:T(8,128)} %fusion.30, bf16[32,256,512]{2,1,0:T(8,128)(2,1)} %get-tuple-element.6), kind=kOutput, calls=%fused_computation.14 | convolution fusion | flops 4303093760 | bytes 41943040 | tf_op jit(solution)/shard_map/ckn,nm->ckm/dot_general | solution.py:29
  611.0 17.4 %convolution_add_fusion = f32[32,256,512]{1,2,0:T(8,128)} fusion(f32[32,256,512]{1,2,0:T(8,128)} %fusion.28, bf16[32,256,512]{2,1,0:T(8,128)(2,1)} %get-tuple-element.5), kind=kOutput, calls=%fused_computation.13 | convolution fusion | flops 4303093760 | bytes 41943040 | tf_op jit(solution)/shard_map/ckn,nm->ckm/dot_general | solution.py:29
  628.3 19.6 %fusion.4 = f32[32,512,256]{2,1,0:T(8,128)} fusion(f32[32,256,512]{1,2,0:T(8,128)} %convolution_add_fusion, f32[32,256,512]{1,2,0:T(8,128)} %convolution_subtract_fusion, f32[256,512]{0,1:T(8,128)S(1)} %get-tuple-element.13, f32[256,512]{0,1:T(8,128)S(1)} %get-tuple-element.14), kind=kOutput, calls=%fused_computation.17 | convolution fusion | flops 2165243904 | bytes 51380224 | tf_op jit(solution)/shard_map/nk,ckm->cnm/dot_general | solution.py:50
  647.9 21.8 %fusion.12 = bf16[32,256,512]{1,2,0:T(8,128)(2,1)} fusion(f32[32,512,256]{2,1,0:T(8,128)} %fusion.4, f32[32,256,512]{1,2,0:T(8,128)} %convolution_subtract_fusion, f32[32,256,512]{1,2,0:T(8,128)} %convolution_add_fusion, f32[256,512]{0,1:T(8,128)S(1)} %get-tuple-element.13, f32[256,512]{0,1:T(8,128)S(1)} %get-tuple-element.14), kind=kOutput, calls=%fused_computation.30 | convolution fusion | flops 2177892352 | bytes 59768832 | tf_op jit(solution)/shard_map/nk,ckm->cnm/dot_general | solution.py:51
  669.7 12.0 %copy.54 = bf16[32,256,512]{2,1,0:T(8,128)(2,1)} copy(bf16[32,256,512]{1,2,0:T(8,128)(2,1)} %fusion.12) | data formatting | bytes 16777216 | tf_op jit(solution)/shard_map/convert_element_type | solution.py:52
  681.7 14.6 %reshape.72 = bf16[32,2,4,16384]{3,2,1,0:T(4,128)(2,1)} reshape(bf16[32,256,512]{2,1,0:T(8,128)(2,1)} %copy.54) | data formatting | bytes 16777216 | tf_op jit(solution)/shard_map/reshape | solution.py:85
  696.2 14.4 %copy.55 = bf16[2,4,1,32,16384]{4,0,3,2,1:T(2,128)(2,1)S(1)} copy(bf16[2,4,1,32,16384]{4,1,0,3,2:T(4,128)(2,1)} %bitcast.86) | data formatting | bytes 16777216 | tf_op jit(solution)/shard_map/reshape | solution.py:86
  710.6 185.3 %all_to_all.40 = bf16[2,4,1,32,16384]{4,0,3,2,1:T(2,128)(2,1)S(1)} all-to-all(bf16[2,4,1,32,16384]{4,0,3,2,1:T(2,128)(2,1)S(1)} %copy.55), channel_id=1, replica_groups=mesh['seg'=8,'tok'=4] {'tok'}, dimensions={1} | all-to-all | bytes 16777216 | tf_op jit(solution)/shard_map/all_to_all | solution.py:87
  895.9 12.8 %fusion.115 = (bf16[1,4,1,32,16384]{4,0,3,2,1:T(2,128)(2,1)}, bf16[1,4,1,32,16384]{4,0,3,2,1:T(2,128)(2,1)S(1)}) fusion(bf16[2,4,1,32,16384]{4,0,3,2,1:T(2,128)(2,1)S(1)} %all_to_all.40), kind=kLoop, calls=%fused_computation.135 | loop fusion | bytes 16777216 | tf_op jit(solution)/shard_map/slice | solution.py:90
  908.7 6.5 copy.70
  917.1 6.7 copy.36
  923.7 8.1 copy.69
  931.9 33.4 %collective-permute-done = bf16[128,16384]{1,0:T(8,128)(2,1)} collective-permute-done((bf16[128,16384]{1,0:T(8,128)(2,1)}, bf16[128,16384]{1,0:T(8,128)(2,1)}, u32[]{:S(2)}, u32[]{:S(2)}) %collective-permute-start) | collective-permute-done | bytes 4194336 | tf_op jit(solution)/shard_map/ppermute | solution.py:15
  (19 shorter events, 33.1 us)
Async XLA Ops:
  19.2 98.3 %all-to-all-start = ((bf16[4,32,16384]{2,1,0:T(8,128)(2,1)}), bf16[4,32,16384]{2,1,0:T(8,128)(2,1)}, u32[]{:S(2)}, u32[]{:S(2)}) async-start(bf16[4,32,16384]{2,1,0:T(8,128)(2,1)} %bitcast.85), calls=%async_computation | async-start | bytes 8388608 | tf_op jit(solution)/shard_map/all_to_all | solution.py:76
  117.6 369.8 %all-to-all-start.1 = ((bf16[2,128,64,512]{3,2,0,1:T(8,128)(2,1)}), bf16[2,128,64,512]{3,2,0,1:T(8,128)(2,1)}, u32[]{:S(2)}, u32[]{:S(2)}) async-start(bf16[2,128,64,512]{3,2,0,1:T(8,128)(2,1)} %bitcast.82), calls=%async_computation.1 | async-start | bytes 33554432 | tf_op jit(solution)/shard_map/all_to_all | solution.py:77
  142.3 10.9 %copy-start.2 = (bf16[32,128,512]{2,1,0:T(8,128)(2,1)S(1)}, bf16[32,128,512]{2,1,0:T(8,128)(2,1)}, u32[]{:S(2)}) copy-start(bf16[32,128,512]{2,1,0:T(8,128)(2,1)} %reshape.71) | copy-start | bytes 12582916
  165.9 15.5 %copy-start = (bf16[32,256,512]{1,2,0:T(8,128)(2,1)S(1)}, bf16[32,256,512]{1,2,0:T(8,128)(2,1)}, u32[]{:S(2)}) copy-start(bf16[32,256,512]{1,2,0:T(8,128)(2,1)} %get-tuple-element.8) | copy-start | bytes 25165828
  566.5 15.5 %copy-start.1 = (bf16[32,256,512]{2,1,0:T(8,128)(2,1)S(1)}, bf16[32,256,512]{2,1,0:T(8,128)(2,1)}, u32[]{:S(2)}) copy-start(bf16[32,256,512]{2,1,0:T(8,128)(2,1)} %get-tuple-element.6) | copy-start | bytes 25165828
  915.2 50.1 %collective-permute-start = (bf16[128,16384]{1,0:T(8,128)(2,1)}, bf16[128,16384]{1,0:T(8,128)(2,1)}, u32[]{:S(2)}, u32[]{:S(2)}) collective-permute-start(bf16[128,16384]{1,0:T(8,128)(2,1)} %bitcast.21), channel_id=1, source_target_pairs={{0,4},{4,8},{8,12},{12,16},{16,20},{20,24},{24,28},{1,5},{5,9},{9,... | collective-permute-start | bytes 12582920 | tf_op jit(solution)/shard_map/ppermute | solution.py:15
  923.7 41.6 %copy-start.3 = (bf16[16384,128]{0,1:T(8,128)(2,1)S(1)}, bf16[16384,128]{0,1:T(8,128)(2,1)}, u32[]{:S(2)}) copy-start(bf16[16384,128]{0,1:T(8,128)(2,1)} %multiply_convert_fusion.1) | copy-start | bytes 12582916
  923.7 41.6 %copy-start.4 = (bf16[16384,128]{0,1:T(8,128)(2,1)S(1)}, bf16[16384,128]{0,1:T(8,128)(2,1)}, u32[]{:S(2)}) copy-start(bf16[16384,128]{0,1:T(8,128)(2,1)} %copy.36) | copy-start | bytes 12582916
  923.7 41.6 %copy-start.5 = (f32[128]{0:T(128)S(1)}, f32[128]{0:T(128)}, u32[]{:S(2)}) copy-start(f32[128]{0:T(128)} %param.9) | copy-start | bytes 1540
where the time goes:
time: 983 us; the launch traced here: 977 us
  waiting for transfers between devices  383 us (39%)
  matrix products  204 us (21%)
  blocking collectives  185 us (19%)
  local copies, waits for them, and re-layouts  164 us (17%)
  other arithmetic  26 us (3%)
  starting transfers between devices  14.3 us (1%)
    all_to_all x1, waiting for transfers between devices, shards(): lax.all_to_all(jnp.transpose(filter_spectrum, (0, 3, 1, 2)), 'tok', split...  279 us
    all_to_all x1, blocking collectives, shards(): lax.all_to_all(grouped, 'tok', split_axis=1, concat_axis=3, tiled=True)  185 us
    dot_general x8, matrix products, einsum_lanes(): jnp.einsum('ckn,nm->ckm', data, table, preferred_element_type=jnp.float32)  139 us
    all_to_all x1, waiting for transfers between devices, shards(): lax.all_to_all(gated.T, 'tok', split_axis=0, concat_axis=1, tiled=True)  70.5 us
    unnamed x18, local copies, waits for them, and re-layouts  57 us
    ppermute x1, waiting for transfers between devices, passed_along(): return lax.ppermute(value, axis, pairs)  33.4 us
    dot_general x1, matrix products, channel_transform(): jnp.einsum('nk,ckm->cnm', inv_nsin, q_imag, preferred_element_type=jnp.fl...  21.8 us
  transfers between devices with their start and end apart: 3, of which 3 were waited for; matrix products, arithmetic and copies ran while one was open for 12% of the time, Pallas kernels for 0%

commit v1 on v0

v1 whole, which is shorter than its diff:
```python
import math

import jax
import jax.numpy as jnp
from jax import lax
from jax.experimental import pallas as pl
from jax.experimental.pallas import tpu as pltpu
from jax.sharding import PartitionSpec as P

N1 = 256
N2 = 512
HALF = N1 // 2
ROWS = HALF + 16
CHUNKS = 2


def span_ids(count):
    return jnp.arange(count, dtype=jnp.int32)


def trig_tables(row_ids, col_ids, modulus):
    product = row_ids[:, None] * col_ids[None, :] % modulus
    angle = product.astype(jnp.float32) * jnp.float32(2.0 * math.pi / modulus)
    return (jnp.cos(angle), jnp.sin(angle))


def half_tables(base):
    rows = span_ids(ROWS)
    k1 = (base + rows) % N1
    used = rows <= HALF
    weight = jnp.where(used, jnp.where((rows == 0) | (rows == HALF), 1.0, 2.0), 0.0)
    weight = weight.astype(jnp.float32) / (N1 * N2)
    cos_one, sin_one = trig_tables(k1, span_ids(HALF), N1)
    forward = jnp.concatenate([cos_one, -sin_one], axis=0).astype(jnp.bfloat16)
    tw = jnp.stack(trig_tables(k1, span_ids(N2), N1 * N2))
    cos_two, sin_two = trig_tables(span_ids(N2), span_ids(N2), N2)
    cos_two = cos_two.astype(jnp.bfloat16)
    sin_two = sin_two.astype(jnp.bfloat16)
    there = jnp.block([[cos_two, -sin_two], [sin_two, cos_two]])
    back = jnp.block([[cos_two, sin_two], [-sin_two, cos_two]])
    inv_cos, inv_sin = trig_tables(span_ids(N1), k1, N1)
    inv_cos = inv_cos.astype(jnp.bfloat16).astype(jnp.float32) * weight[None, :]
    inv_sin = inv_sin.astype(jnp.bfloat16).astype(jnp.float32) * weight[None, :]
    inverse = jnp.concatenate([inv_cos, -inv_sin], axis=1).astype(jnp.bfloat16)
    return forward, tw, there, back, inverse


def conv_kernel(x_ref, h_ref, fwd_ref, tw_ref, there_ref, back_ref, inv_ref, main_ref, tail_ref):
    f32 = jnp.float32
    data = x_ref[:, 0].astype(f32).reshape(HALF, N2).astype(jnp.bfloat16)
    a = jnp.dot(fwd_ref[...], data, preferred_element_type=f32)
    a_re, a_im = a[:ROWS], a[ROWS:]
    tc, ts = tw_ref[0], tw_ref[1]
    b_re = (a_re * tc + a_im * ts).astype(jnp.bfloat16)
    b_im = (a_im * tc - a_re * ts).astype(jnp.bfloat16)
    spec = jnp.dot(
        jnp.concatenate([b_re, b_im], axis=1), there_ref[...], preferred_element_type=f32
    )
    s_re, s_im = spec[:, :N2], spec[:, N2:]
    h_re = h_ref[0, 0].astype(f32)
    h_im = h_ref[0, 1].astype(f32)
    z_re = (s_re * h_re - s_im * h_im).astype(jnp.bfloat16)
    z_im = (s_re * h_im + s_im * h_re).astype(jnp.bfloat16)
    p = jnp.dot(jnp.concatenate([z_re, z_im], axis=1), back_ref[...], preferred_element_type=f32)
    p_re, p_im = p[:, :N2], p[:, N2:]
    q_re = (p_re * tc - p_im * ts).astype(jnp.bfloat16)
    q_im = (p_im * tc + p_re * ts).astype(jnp.bfloat16)
    conv = jnp.dot(inv_ref[...], jnp.concatenate([q_re, q_im], axis=0), preferred_element_type=f32)
    shape = main_ref.shape
    main_ref[...] = conv[:HALF].reshape(shape).astype(jnp.bfloat16)
    tail_ref[...] = conv[HALF:].reshape(shape).astype(jnp.bfloat16)


def conv_call(x, h, tables):
    parts, count, rows, _ = x.shape
    block = pl.BlockSpec((parts, 1, rows, N2), lambda c: (0, c, 0, 0))
    whole = lambda t: pl.BlockSpec(t.shape, lambda c: (0,) * t.ndim)
    out = jax.ShapeDtypeStruct(x.shape, jnp.bfloat16)
    flops = 4 * count * ROWS * N2 * (HALF + 2 * N2 + 2 * N2 + N1)
    return pl.pallas_call(
        conv_kernel,
        grid=(count,),
        in_specs=[block, pl.BlockSpec((1, 2, ROWS, N2), lambda c: (c, 0, 0, 0))]
        + [whole(t) for t in tables],
        out_specs=[block, block],
        out_shape=[out, out],
        compiler_params=pltpu.CompilerParams(vmem_limit_bytes=48 * 1024 * 1024),
        cost_estimate=pl.CostEstimate(
            flops=flops, bytes_accessed=6 * x.size + 2 * h.size, transcendentals=0
        ),
    )(x, h, *tables)


def half_filter(filt, narrow):
    toks, segs = lax.axis_size("tok"), lax.axis_size("seg")
    tok, seg = lax.axis_index("tok"), lax.axis_index("seg")
    rows = filt.shape[1]
    channels = filt.shape[3]
    share = rows // segs
    side = toks // 2
    upper = tok // side
    mine = lax.dynamic_slice(
        filt, (0, seg * share, 0, upper * (channels // 2)), (2, share, N2, channels // 2)
    )
    mine = jnp.transpose(mine, (3, 0, 1, 2)).reshape(side, narrow, 2, share, N2)
    groups = [list(range(side)), list(range(side, toks))]
    mine = lax.all_to_all(mine, "tok", 0, 0, axis_index_groups=groups, tiled=True)
    both = lax.all_gather(mine, "seg")
    both = jnp.transpose(both, (2, 3, 1, 0, 4, 5)).reshape(narrow, 2, HALF, N2)
    first = jnp.transpose(filt[:, 0], (2, 0, 1)).reshape(toks, narrow, 2, N2)
    first = lax.all_to_all(first, "tok", 0, 0, tiled=True)
    last = lax.dynamic_index_in_dim(first, (1 - upper) * side, 0, keepdims=False)
    last = jnp.pad(last[:, :, None], ((0, 0), (0, 0), (0, ROWS - HALF - 1), (0, 0)))
    return jnp.concatenate([both, last], axis=2)


def shards(value, gate_in, gate_out, filter_spectrum, skip_gain):
    f32 = jnp.float32
    toks, segs = lax.axis_size("tok"), lax.axis_size("seg")
    gated = (value.astype(f32) * gate_in.astype(f32)).astype(jnp.bfloat16)
    tokens, channels = gated.shape
    narrow = channels // toks
    rows = tokens // N2
    step = narrow // CHUNKS
    upper = lax.axis_index("tok") // (toks // 2)
    tables = half_tables(upper * HALF)
    turned = jnp.transpose(gated.reshape(rows, N2, channels), (2, 0, 1))
    turned = turned.reshape(toks, narrow, rows, N2)
    filt = half_filter(filter_spectrum, narrow)
    onward = [(i, i + 1) for i in range(segs - 1)]
    pieces = []
    for at in range(CHUNKS):
        span = slice(at * step, (at + 1) * step)
        x = lax.all_to_all(turned[:, span], "tok", 0, 0, tiled=True)
        main, tail = conv_call(x, filt[span], tables)
        carried = lax.ppermute(tail, "seg", onward)
        mixed = (main.astype(f32) + carried.astype(f32)).astype(jnp.bfloat16)
        pieces.append(lax.all_to_all(mixed, "tok", 0, 0, tiled=True))
    mixed = jnp.concatenate(pieces, axis=1).reshape(channels, rows, N2)
    mixed = jnp.transpose(mixed, (1, 2, 0)).reshape(tokens, channels)
    result = gate_out.astype(f32) * (mixed.astype(f32) + skip_gain[None, :] * gated.astype(f32))
    return result.astype(jnp.bfloat16)


def solution(mesh):
    return jax.shard_map(
        shards,
        mesh=mesh,
        in_specs=(
            P(("seg", "tok"), None),
            P(("seg", "tok"), None),
            P(("seg", "tok"), None),
            P(None, "tok", None, None),
            P(),
        ),
        out_specs=P(("seg", "tok"), None),
        check_vma=False,
    )
```

time: 983 us -> 312 us (0.32)
  waiting for transfers between devices: 383 us -> 54.5 us
  matrix products: 204 us -> 0 us
  local copies, waits for them, and re-layouts: 164 us -> 44.3 us
  blocking collectives: 185 us -> 70 us
  Pallas kernels: 0 us -> 51.3 us
  other arithmetic: 26 us -> 54.3 us
  between operations: 0.33 us -> 13.6 us
    all_to_all x2 -> x4, waiting for transfers between devices: 349 us -> 0.01 us  [the longest x2 0.01 us: shards(): x = lax.all_to_all(turned[:, span], 'tok', 0, 0, tiled=True)]
    dot_general x12 -> x0, matrix products: 204 us -> none  [the longest x8 139 us: einsum_lanes(): jnp.einsum('ckn,nm->ckm', data, table, preferred_element_type=jnp.float32)]
    all_to_all x1 -> x2, blocking collectives: 185 us -> 70 us  [the longest x1 52.9 us: shards(): pieces.append(lax.all_to_all(mixed, 'tok', 0, 0, tiled=True))]
    unnamed x18 -> x6, local copies, waits for them, and re-layouts: 57 us -> 1.74 us
    pallas_call x0 -> x2, Pallas kernels: none -> 51.3 us  [conv_call(): pl.pallas_call(conv_kernel, grid=(count,), in_specs=[block, pl.BlockSpec(...]
    reshape x3 -> x2, local copies, waits for them, and re-layouts: 36.7 us -> 8.64 us  [the longest x1 7.89 us: shards(): turned = jnp.transpose(gated.reshape(rows, N2, channels), (2, 0, 1))]
    convert_element_type x4 -> x2, local copies, waits for them, and re-layouts: 36.6 us -> 10.1 us  [the longest x1 10 us: shards(): mixed.astype(f32) + skip_gain[None, :] * gated.astype(f32)]
    all_to_all x2 -> x0, local copies, waits for them, and re-layouts: 21.4 us -> none  [the longest x1 14 us: shards(): lax.all_to_all(jnp.transpose(filter_spectrum, (0, 3, 1, 2)), 'tok', split...]
  transfers between devices with their start and end apart: 3 -> 7, of which waited for: 3 -> 3; matrix products, arithmetic and copies ran while one was open for 12% -> 22% of each run, Pallas kernels for 0% -> 16%
where the time goes in v1:
time: 312 us; the launch traced here: 311 us
  blocking collectives  70 us (22%)
  waiting for transfers between devices  54.5 us (17%)
  other arithmetic  54.3 us (17%)
  Pallas kernels  51.3 us (16%)
  local copies, waits for them, and re-layouts  44.3 us (14%)
  starting transfers between devices  23.1 us (7%)
  between operations  13.6 us (4%)
    all_to_all x1, blocking collectives, shards(): pieces.append(lax.all_to_all(mixed, 'tok', 0, 0, tiled=True))  52.9 us
    pallas_call x2, Pallas kernels, conv_call(): pl.pallas_call(conv_kernel, grid=(count,), in_specs=[block, pl.BlockSpec(...  51.3 us
    ppermute x2, waiting for transfers between devices, shards(): carried = lax.ppermute(tail, 'seg', onward)  50.5 us
    all_to_all x1, blocking collectives, half_filter(): lax.all_to_all(mine, 'tok', 0, 0, axis_index_groups=groups, tiled=True)  17.2 us
    concatenate x1, other arithmetic, half_tables(): back = jnp.block([[cos_two, sin_two], [-sin_two, cos_two]])  10.2 us
    convert_element_type x1, local copies, waits for them, and re-layouts, shards(): mixed.astype(f32) + skip_gain[None, :] * gated.astype(f32)  10 us
    all_to_all x2, starting transfers between devices, shards(): x = lax.all_to_all(turned[:, span], 'tok', 0, 0, tiled=True)  9.96 us
    convert_element_type x1, other arithmetic, shards(): return result.astype(jnp.bfloat16)  8.72 us
  transfers between devices with their start and end apart: 7, of which 3 were waited for; matrix products, arithmetic and copies ran while one was open for 22% of the time, Pallas kernels for 16%

profile of v1, /device:TPU:2, one launch (start us, length us, event | category | flops | bytes accessed | tf_op | source)
XLA Modules:
  0.0 311.1 jit_solution(815249916866724819)
XLA Ops:
  6.5 2.2 constant_dynamic-slice_fusion
  8.8 1.6 copy.30
  10.4 17.2 %all_to_all.30 = bf16[2,32,2,8,512]{4,3,2,1,0:T(8,128)(2,1)} all-to-all(bf16[2,32,2,8,512]{4,3,2,1,0:T(8,128)(2,1)S(1)} %bitcast.33), channel_id=1, replica_groups={{0,1},{2,3},{4,5},{6,7},{8,9},{10,11},{12,13},{14,15},{16,17},{18,19},{..., dimensions={0} | all-to-all | bytes 2097152 | tf_op jit(solution)/shard_map/all_to_all | solution.py:107
  28.5 3.9 %all-to-all-start.2 = ((bf16[4,32,2,512]{3,1,2,0:T(8,128)(2,1)}), bf16[4,32,2,512]{3,1,2,0:T(8,128)(2,1)S(1)}, u32[]{:S(2)}, u32[]{:S(2)}) async-start(bf16[4,32,2,512]{3,1,2,0:T(8,128)(2,1)} %copy.26), calls=%async_computation.2 | async-start | bytes 524288 | tf_op jit(solution)/shard_map/all_to_all | solution.py:111
  32.5 6.1 %multiply_convert_fusion = bf16[16384,128]{1,0:T(8,128)(2,1)} fusion(bf16[16384,128]{1,0:T(8,128)(2,1)} %param.6, bf16[16384,128]{1,0:T(8,128)(2,1)} %param.5), kind=kLoop, calls=%fused_computation.7 | loop fusion | flops 8388608 | bytes 12582912 | tf_op jit(solution)/shard_map/convert_element_type | solution.py:120
  39.1 7.9 %copy.22 = bf16[32,512,128]{1,0,2:T(8,128)(2,1)} copy(bf16[32,512,128]{2,1,0:T(8,128)(2,1)} %bitcast.29) | data formatting | bytes 8388608 | tf_op jit(solution)/shard_map/reshape | solution.py:127
  47.0 4.9 %fusion.38 = (bf16[4,16,32,512]{3,2,1,0:T(8,128)(2,1)}, bf16[4,16,32,512]{3,2,1,0:T(8,128)(2,1)}) fusion(bf16[4,32,32,512]{3,2,1,0:T(8,128)(2,1)} %bitcast.31), kind=kLoop, calls=%fused_computation.80 | loop fusion | bytes 8388608 | tf_op jit(solution)/shard_map/slice | solution.py:134
  51.9 5.4 %all-to-all-start.4 = ((bf16[4,16,32,512]{3,2,1,0:T(8,128)(2,1)}), bf16[4,16,32,512]{3,2,1,0:T(8,128)(2,1)S(1)}, u32[]{:S(2)}, u32[]{:S(2)}) async-start(bf16[4,16,32,512]{3,2,1,0:T(8,128)(2,1)} %get-tuple-element.16), calls=%async_computation.4 | async-start | bytes 4194304 | tf_op jit(solution)/shard_map/all_to_all | solution.py:134
  57.3 1.0 multiply_convert_fusion.1
  58.4 4.0 %fusion.18 = bf16[512,512]{1,0:T(8,128)(2,1)S(1)} fusion(), kind=kLoop, calls=%fused_computation.45 | loop fusion | flops 4718592 | bytes 524288 | tf_op jit(solution)/shard_map/neg | solution.py:39
  62.4 1.2 fusion.24
  63.7 4.3 %sine_convert_fusion = (bf16[512,512]{1,0:T(8,128)(2,1)S(1)}, bf16[512,512]{1,0:T(8,128)(2,1)S(1)}) fusion(), kind=kLoop, calls=%fused_computation.23 | loop fusion | flops 4194304 | bytes 1048576 | tf_op jit(solution)/shard_map/convert_element_type | solution.py:38
  68.0 10.2 %fusion.5 = (bf16[1024,1024]{1,0:T(8,128)(2,1)}, bf16[1024,1024]{1,0:T(8,128)(2,1)}) fusion(bf16[512,512]{1,0:T(8,128)(2,1)S(1)} %get-tuple-element.26, bf16[512,512]{1,0:T(8,128)(2,1)S(1)} %fusion.18, bf16[512,512]{1,0:T(8,128)(2,1)S(1)} %get-tuple-element.25), kind=kLoop, calls=%fused_computation.16 | loop fusion | flops 14680064 | bytes 5767168 | tf_op jit(solution)/shard_map/jit(block)/concatenate | solution.py:40
  78.3 4.0 %all-gather.3.cloned.1.call-done = bf16[16,32,2,8,512]{4,3,2,1,0:T(8,128)(2,1)} async-done(((bf16[2,32,2,8,512]{4,3,2,1,0:T(8,128)(2,1)}), bf16[16,32,2,8,512]{4,3,2,1,0:T(8,128)(2,1)}) %all-gather.3.cloned.1.call-update) | async-done | bytes 8388624 | tf_op jit(solution)/shard_map/all_gather | solution.py:108
  82.3 8.0 %copy.24 = bf16[32,2,2,8,8,512]{5,4,3,2,1,0:T(8,128)(2,1)} copy(bf16[32,2,2,8,8,512]{5,4,1,0,2,3:T(8,128)(2,1)} %bitcast.32) | data formatting | bytes 16777216 | tf_op jit(solution)/shard_map/transpose | solution.py:109
  90.3 8.3 %fusion.1 = bf16[32,2,144,512]{3,2,1,0:T(8,128)(2,1)} fusion(bf16[32,2,1,512]{3,2,1,0:T(2,128)(2,1)S(1)} %copy.27, bf16[32,2,128,512]{3,2,1,0:T(8,128)(2,1)} %bitcast.30), kind=kLoop, calls=%fused_computation.2 | loop fusion | flops 28311552 | bytes 17891328 | tf_op jit(solution)/shard_map/concatenate | solution.py:114
  98.7 8.5 %fusion.37 = (bf16[16,2,144,512]{3,2,1,0:T(8,128)(2,1)}, bf16[16,2,144,512]{3,2,1,0:T(8,128)(2,1)}) fusion(bf16[32,2,144,512]{3,2,1,0:T(8,128)(2,1)} %fusion.1), kind=kLoop, calls=%fused_computation.79 | loop fusion | bytes 18874368 | tf_op jit(solution)/shard_map/slice | solution.py:135
  107.2 4.6 %all-to-all-start = ((bf16[4,16,32,512]{3,2,1,0:T(8,128)(2,1)}), bf16[4,16,32,512]{3,2,1,0:T(8,128)(2,1)}, u32[]{:S(2)}, u32[]{:S(2)}) async-start(bf16[4,16,32,512]{3,2,1,0:T(8,128)(2,1)} %get-tuple-element.15), calls=%async_computation | async-start | bytes 4194304 | tf_op jit(solution)/shard_map/all_to_all | solution.py:134
  111.8 25.6 %shard_map.56 = (bf16[4,16,32,512]{3,2,1,0:T(8,128)(2,1)S(1)}, bf16[4,16,32,512]{3,2,1,0:T(8,128)(2,1)S(1)}) custom-call(bf16[4,16,32,512]{3,2,1,0:T(8,128)(2,1)} %copy-done, bf16[16,2,144,512]{3,2,1,0:T(8,128)(2,1)} %get-tuple-element.14.h_ref, bf16[288,128]{1,0:T(8,128)(2,1)S(1)} %pad_maximum_fusion.7.fwd_ref, ...), custom_call_target="tpu_custom_call" | custom-call | flops 11475615744 | bytes 11010048 | tf_op jit(solution)/shard_map/pallas_call | solution.py:80
  137.4 2.3 collective-permute-start.1
  139.7 25.1 %collective-permute-done.1 = bf16[4,16,32,512]{3,2,1,0:T(8,128)(2,1)S(1)} collective-permute-done((bf16[4,16,32,512]{3,2,1,0:T(8,128)(2,1)S(1)}, bf16[4,16,32,512]{3,2,1,0:T(8,128)(2,1)S(1)}, u32[]{:S(2)}, u32[]{:S(2)}) %collective-permute-start.1) | collective-permute-done | bytes 2097184 | tf_op jit(solution)/shard_map/ppermute | solution.py:136
  164.8 2.3 add_convert_fusion
  167.0 5.1 %all-to-all-start.5 = ((bf16[4,16,32,512]{3,2,1,0:T(8,128)(2,1)}), bf16[4,16,32,512]{3,2,1,0:T(8,128)(2,1)}, u32[]{:S(2)}, u32[]{:S(2)}) async-start(bf16[4,16,32,512]{3,2,1,0:T(8,128)(2,1)} %add_convert_fusion), calls=%async_computation.5 | async-start | bytes 4194304 | tf_op jit(solution)/shard_map/all_to_all | solution.py:138
  172.1 25.6 %shard_map.55 = (bf16[4,16,32,512]{3,2,1,0:T(8,128)(2,1)S(1)}, bf16[4,16,32,512]{3,2,1,0:T(8,128)(2,1)S(1)}) custom-call(bf16[4,16,32,512]{3,2,1,0:T(8,128)(2,1)} %all-to-all-done.x_ref, bf16[16,2,144,512]{3,2,1,0:T(8,128)(2,1)} %get-tuple-element.13.h_ref, bf16[288,128]{1,0:T(8,128)(2,1)S(1)} %pad_maximum_fusion.7.fwd_ref, ...), custom_call_target="tpu_custom_call" | custom-call | flops 11475615744 | bytes 11010048 | tf_op jit(solution)/shard_map/pallas_call | solution.py:80
  197.8 1.9 collective-permute-start
  199.7 25.4 %collective-permute-done = bf16[4,16,32,512]{3,2,1,0:T(8,128)(2,1)S(1)} collective-permute-done((bf16[4,16,32,512]{3,2,1,0:T(8,128)(2,1)S(1)}, bf16[4,16,32,512]{3,2,1,0:T(8,128)(2,1)S(1)}, u32[]{:S(2)}, u32[]{:S(2)}) %collective-permute-start) | collective-permute-done | bytes 2097184 | tf_op jit(solution)/shard_map/ppermute | solution.py:136
  225.1 0.8 add_convert_fusion.1
  225.9 52.9 %all_to_all.31 = bf16[4,16,32,512]{3,2,1,0:T(8,128)(2,1)S(1)} all-to-all(bf16[4,16,32,512]{3,2,1,0:T(8,128)(2,1)S(1)} %add_convert_fusion.1), channel_id=1, replica_groups=mesh['seg'=8,'tok'=4] {'tok'}, dimensions={0} | all-to-all | bytes 4194304 | tf_op jit(solution)/shard_map/all_to_all | solution.py:138
  278.8 2.0 pad_maximum_fusion
  280.8 4.7 %convert_bitcast_fusion = f32[32,512,128]{1,0,2:T(8,128)} fusion(bf16[4,32,32,512]{3,2,1,0:T(8,128)(2,1)S(1)} %pad_maximum_fusion), kind=kLoop, calls=%fused_computation.3 | loop fusion | flops 2097152 | bytes 12582912 | tf_op jit(solution)/shard_map/convert_element_type | solution.py:141
  285.5 10.0 %copy.29 = f32[32,512,128]{2,1,0:T(8,128)} copy(f32[32,512,128]{1,0,2:T(8,128)} %convert_bitcast_fusion) | data formatting | bytes 16777216 | tf_op jit(solution)/shard_map/convert_element_type | solution.py:141
  295.6 8.7 %fusion.3 = bf16[16384,128]{1,0:T(8,128)(2,1)} fusion(f32[32,512,128]{2,1,0:T(8,128)} %copy.29, bf16[16384,128]{1,0:T(8,128)(2,1)} %multiply_convert_fusion, bf16[16384,128]{1,0:T(8,128)(2,1)} %param.7, f32[128]{0:T(128)S(1)} %copy-done.1), kind=kLoop, calls=%fused_computation.6 | loop fusion | flops 12582912 | bytes 20972032 | tf_op jit(solution)/shard_map/convert_element_type | solution.py:142
  (24 shorter events, 1.8 us)
Async XLA Ops:
  6.5 75.8 %all-gather.3.cloned.1.call-start = ((), (), s32[]{:S(2)}) async-start(), calls=%async_computation.6 | async-start | bytes 9437184 | tf_op jit(solution)/shard_map/all_gather | solution.py:108
  8.8 18.8 %slice-start = ((bf16[2,64,512,128]{3,2,1,0:T(8,128)(2,1)}), bf16[2,1,512,128]{3,2,1,0:T(8,128)(2,1)S(1)}, s32[]{:S(2)}) async-start(bf16[2,64,512,128]{3,2,1,0:T(8,128)(2,1)} %param.8), calls=%async_computation.7 | async-start | bytes 524288 | tf_op jit(solution)/shard_map/slice | solution.py:110
  28.5 23.4 %all-to-all-start.2 = ((bf16[4,32,2,512]{3,1,2,0:T(8,128)(2,1)}), bf16[4,32,2,512]{3,1,2,0:T(8,128)(2,1)S(1)}, u32[]{:S(2)}, u32[]{:S(2)}) async-start(bf16[4,32,2,512]{3,1,2,0:T(8,128)(2,1)} %copy.26), calls=%async_computation.2 | async-start | bytes 524288 | tf_op jit(solution)/shard_map/all_to_all | solution.py:111
  51.9 55.3 %all-to-all-start.4 = ((bf16[4,16,32,512]{3,2,1,0:T(8,128)(2,1)}), bf16[4,16,32,512]{3,2,1,0:T(8,128)(2,1)S(1)}, u32[]{:S(2)}, u32[]{:S(2)}) async-start(bf16[4,16,32,512]{3,2,1,0:T(8,128)(2,1)} %get-tuple-element.16), calls=%async_computation.4 | async-start | bytes 4194304 | tf_op jit(solution)/shard_map/all_to_all | solution.py:134
  107.2 4.6 %copy-start = (bf16[4,16,32,512]{3,2,1,0:T(8,128)(2,1)}, bf16[4,16,32,512]{3,2,1,0:T(8,128)(2,1)S(1)}, u32[]{:S(2)}) copy-start(bf16[4,16,32,512]{3,2,1,0:T(8,128)(2,1)S(1)} %all-to-all-done.4.x_ref) | copy-start | bytes 6291460
  107.2 59.8 %all-to-all-start = ((bf16[4,16,32,512]{3,2,1,0:T(8,128)(2,1)}), bf16[4,16,32,512]{3,2,1,0:T(8,128)(2,1)}, u32[]{:S(2)}, u32[]{:S(2)}) async-start(bf16[4,16,32,512]{3,2,1,0:T(8,128)(2,1)} %get-tuple-element.15), calls=%async_computation | async-start | bytes 4194304 | tf_op jit(solution)/shard_map/all_to_all | solution.py:134
  137.4 27.4 %collective-permute-start.1 = (bf16[4,16,32,512]{3,2,1,0:T(8,128)(2,1)S(1)}, bf16[4,16,32,512]{3,2,1,0:T(8,128)(2,1)S(1)}, u32[]{:S(2)}, u32[]{:S(2)}) collective-permute-start(bf16[4,16,32,512]{3,2,1,0:T(8,128)(2,1)S(1)} %get-tuple-element.12), channel_id=1, source_target_pairs={{0,4},{4,8},{8,12},{12,16},{16,20},{20,24},{24,28},{1,5},{5,9},{9,... | collective-permute-start | bytes 6291464 | tf_op jit(solution)/shard_map/ppermute | solution.py:136
  167.0 58.9 %all-to-all-start.5 = ((bf16[4,16,32,512]{3,2,1,0:T(8,128)(2,1)}), bf16[4,16,32,512]{3,2,1,0:T(8,128)(2,1)}, u32[]{:S(2)}, u32[]{:S(2)}) async-start(bf16[4,16,32,512]{3,2,1,0:T(8,128)(2,1)} %add_convert_fusion), calls=%async_computation.5 | async-start | bytes 4194304 | tf_op jit(solution)/shard_map/all_to_all | solution.py:138
  197.8 27.4 %collective-permute-start = (bf16[4,16,32,512]{3,2,1,0:T(8,128)(2,1)S(1)}, bf16[4,16,32,512]{3,2,1,0:T(8,128)(2,1)S(1)}, u32[]{:S(2)}, u32[]{:S(2)}) collective-permute-start(bf16[4,16,32,512]{3,2,1,0:T(8,128)(2,1)S(1)} %get-tuple-element.10), channel_id=1, source_target_pairs={{0,4},{4,8},{8,12},{12,16},{16,20},{20,24},{24,28},{1,5},{5,9},{9,... | collective-permute-start | bytes 6291464 | tf_op jit(solution)/shard_map/ppermute | solution.py:136
  285.5 10.0 %copy-start.1 = (f32[128]{0:T(128)S(1)}, f32[128]{0:T(128)}, u32[]{:S(2)}) copy-start(f32[128]{0:T(128)} %param.9) | copy-start | bytes 1540
Sparse Core Ops, SparseCore 0:
  27.7 54.5 all-gather.2

commit v2 on v1

v2 whole, which is shorter than its diff:
```python
import math

import jax
import jax.numpy as jnp
from jax import lax
from jax.experimental import pallas as pl
from jax.experimental.pallas import tpu as pltpu
from jax.sharding import PartitionSpec as P

N1 = 256
N2 = 512
HALF = N1 // 2
ROWS = HALF + 16
CHUNKS = 2
LINES = 16
GROUP = 4


def span_ids(count):
    return jnp.arange(count, dtype=jnp.int32)


def trig_tables(row_ids, col_ids, modulus):
    product = row_ids[:, None] * col_ids[None, :] % modulus
    angle = product.astype(jnp.float32) * jnp.float32(2.0 * math.pi / modulus)
    return (jnp.cos(angle), jnp.sin(angle))


def half_tables(base):
    rows = span_ids(ROWS)
    k1 = (base + rows) % N1
    used = rows <= HALF
    weight = jnp.where(used, jnp.where((rows == 0) | (rows == HALF), 1.0, 2.0), 0.0)
    weight = weight.astype(jnp.float32) / (N1 * N2)
    cos_one, sin_one = trig_tables(k1, span_ids(HALF), N1)
    forward = jnp.concatenate([cos_one, -sin_one], axis=0).astype(jnp.bfloat16)
    tw = jnp.stack(trig_tables(k1, span_ids(N2), N1 * N2))
    cos_two, sin_two = trig_tables(span_ids(N2), span_ids(N2), N2)
    cos_two = cos_two.astype(jnp.bfloat16)
    sin_two = sin_two.astype(jnp.bfloat16)
    there = jnp.block([[cos_two, -sin_two], [sin_two, cos_two]])
    back = jnp.block([[cos_two, sin_two], [-sin_two, cos_two]])
    inv_cos, inv_sin = trig_tables(span_ids(N1), k1, N1)
    inv_cos = inv_cos.astype(jnp.bfloat16).astype(jnp.float32) * weight[None, :]
    inv_sin = inv_sin.astype(jnp.bfloat16).astype(jnp.float32) * weight[None, :]
    inverse = jnp.concatenate([inv_cos, -inv_sin], axis=1).astype(jnp.bfloat16)
    return forward, tw, there, back, inverse


def turn_kernel(value_ref, gate_ref, *out_refs):
    f32 = jnp.float32
    gated = (value_ref[...].astype(f32) * gate_ref[...].astype(f32)).astype(jnp.bfloat16)
    lines = gated.shape[0] // N2
    turned = [gated[i * N2 : (i + 1) * N2].T for i in range(lines)]
    toks, step, _, _ = out_refs[0].shape
    turned = jnp.stack([t.astype(f32) for t in turned], axis=1).astype(jnp.bfloat16)
    turned = turned.reshape(toks, step * len(out_refs), lines, N2)
    for at, out_ref in enumerate(out_refs):
        out_ref[...] = turned[:, at * step : (at + 1) * step]


def turn_call(value, gate, toks):
    tokens, channels = value.shape
    rows = tokens // N2
    lines = min(rows, LINES)
    step = channels // toks // CHUNKS
    flat = pl.BlockSpec((lines * N2, channels), lambda i: (i, 0))
    out = jax.ShapeDtypeStruct((toks, step, rows, N2), jnp.bfloat16)
    return pl.pallas_call(
        turn_kernel,
        grid=(rows // lines,),
        in_specs=[flat, flat],
        out_specs=[pl.BlockSpec((toks, step, lines, N2), lambda i: (0, 0, i, 0))] * CHUNKS,
        out_shape=[out] * CHUNKS,
        compiler_params=pltpu.CompilerParams(vmem_limit_bytes=48 * 1024 * 1024),
        cost_estimate=pl.CostEstimate(
            flops=value.size, bytes_accessed=6 * value.size, transcendentals=0
        ),
    )(value, gate)


def finish_kernel(value_ref, gate_ref, gate_out_ref, skip_ref, *refs):
    f32 = jnp.float32
    out_ref = refs[-1]
    toks, step, lines, _ = refs[0].shape
    channels = out_ref.shape[1]
    mixed = jnp.concatenate([r[...] for r in refs[:-1]], axis=1).astype(f32)
    mixed = mixed.reshape(channels, lines, N2)
    for i in range(lines):
        span = slice(i * N2, (i + 1) * N2)
        line = mixed[:, i].astype(jnp.bfloat16).T.astype(f32)
        gated = value_ref[span].astype(f32) * gate_ref[span].astype(f32)
        gated = gated.astype(jnp.bfloat16).astype(f32)
        line = gate_out_ref[span].astype(f32) * (line + skip_ref[...] * gated)
        out_ref[span] = line.astype(jnp.bfloat16)


def finish_call(value, gate, gate_out, skip, pieces):
    tokens, channels = value.shape
    toks, step, rows, _ = pieces[0].shape
    lines = min(rows, LINES)
    flat = pl.BlockSpec((lines * N2, channels), lambda i: (i, 0))
    piece = pl.BlockSpec((toks, step, lines, N2), lambda i: (0, 0, i, 0))
    return pl.pallas_call(
        finish_kernel,
        grid=(rows // lines,),
        in_specs=[flat] * 3 + [pl.BlockSpec((1, channels), lambda i: (0, 0))] + [piece] * len(pieces),
        out_specs=flat,
        out_shape=jax.ShapeDtypeStruct(value.shape, jnp.bfloat16),
        compiler_params=pltpu.CompilerParams(vmem_limit_bytes=48 * 1024 * 1024),
        cost_estimate=pl.CostEstimate(
            flops=4 * value.size, bytes_accessed=10 * value.size, transcendentals=0
        ),
    )(value, gate, gate_out, skip[None, :], *pieces)


def conv_kernel(x_ref, h_ref, fwd_ref, tw_ref, there_ref, back_ref, inv_ref, main_ref, tail_ref):
    f32 = jnp.float32
    toks, count, rows, _ = x_ref.shape
    tc, ts = tw_ref[0], tw_ref[1]
    b = []
    for i in range(count):
        data = x_ref[:, i].astype(f32).reshape(HALF, N2).astype(jnp.bfloat16)
        a = jnp.dot(fwd_ref[...], data, preferred_element_type=f32)
        a_re, a_im = a[:ROWS], a[ROWS:]
        b_re = (a_re * tc + a_im * ts).astype(jnp.bfloat16)
        b_im = (a_im * tc - a_re * ts).astype(jnp.bfloat16)
        b.append(jnp.concatenate([b_re, b_im], axis=1))
    b = jnp.concatenate(b, axis=0)
    spec = jnp.dot(b, there_ref[...], preferred_element_type=f32)
    z = []
    for i in range(count):
        part = spec[i * ROWS : (i + 1) * ROWS]
        s_re, s_im = part[:, :N2], part[:, N2:]
        h_re = h_ref[i, 0].astype(f32)
        h_im = h_ref[i, 1].astype(f32)
        z_re = (s_re * h_re - s_im * h_im).astype(jnp.bfloat16)
        z_im = (s_re * h_im + s_im * h_re).astype(jnp.bfloat16)
        z.append(jnp.concatenate([z_re, z_im], axis=1))
    z = jnp.concatenate(z, axis=0)
    p = jnp.dot(z, back_ref[...], preferred_element_type=f32)
    for i in range(count):
        part = p[i * ROWS : (i + 1) * ROWS]
        p_re, p_im = part[:, :N2], part[:, N2:]
        q_re = (p_re * tc - p_im * ts).astype(jnp.bfloat16)
        q_im = (p_im * tc + p_re * ts).astype(jnp.bfloat16)
        q = jnp.concatenate([q_re, q_im], axis=0)
        conv = jnp.dot(inv_ref[...], q, preferred_element_type=f32)
        main_ref[:, i] = conv[:HALF].reshape(toks, rows, N2).astype(jnp.bfloat16)
        tail_ref[:, i] = conv[HALF:].reshape(toks, rows, N2).astype(jnp.bfloat16)


def conv_call(x, h, tables):
    parts, count, rows, _ = x.shape
    group = min(count, GROUP)
    block = pl.BlockSpec((parts, group, rows, N2), lambda c: (0, c, 0, 0))
    whole = lambda t: pl.BlockSpec(t.shape, lambda c: (0,) * t.ndim)
    out = jax.ShapeDtypeStruct(x.shape, jnp.bfloat16)
    flops = 4 * count * ROWS * N2 * (HALF + 2 * N2 + 2 * N2 + N1)
    return pl.pallas_call(
        conv_kernel,
        grid=(count // group,),
        in_specs=[block, pl.BlockSpec((group, 2, ROWS, N2), lambda c: (c, 0, 0, 0))]
        + [whole(t) for t in tables],
        out_specs=[block, block],
        out_shape=[out, out],
        compiler_params=pltpu.CompilerParams(vmem_limit_bytes=48 * 1024 * 1024),
        cost_estimate=pl.CostEstimate(
            flops=flops, bytes_accessed=6 * x.size + 2 * h.size, transcendentals=0
        ),
    )(x, h, *tables)


def half_filter(filt, narrow):
    toks, segs = lax.axis_size("tok"), lax.axis_size("seg")
    tok, seg = lax.axis_index("tok"), lax.axis_index("seg")
    rows = filt.shape[1]
    channels = filt.shape[3]
    share = rows // segs
    side = toks // 2
    upper = tok // side
    mine = lax.dynamic_slice(
        filt, (0, seg * share, 0, upper * (channels // 2)), (2, share, N2, channels // 2)
    )
    mine = jnp.transpose(mine, (3, 0, 1, 2)).reshape(side, narrow, 2, share, N2)
    own = tok % side
    parts = []
    for by in range(side):
        part = lax.dynamic_index_in_dim(mine, (own + side - by) % side, 0, keepdims=False)
        if by:
            pairs = [(t, t // side * side + (t + side - by) % side) for t in range(toks)]
            part = lax.ppermute(part, "tok", pairs)
        parts.append(part)
    mine = jnp.stack(parts)
    mine = jnp.take(mine, (span_ids(side) - own) % side, axis=0) if side > 2 else jnp.where(
        own == 0, mine, mine[::-1]
    )
    both = lax.all_gather(mine, "seg")
    both = jnp.transpose(both, (2, 3, 1, 0, 4, 5)).reshape(narrow, 2, HALF, N2)
    first = jnp.transpose(filt[:, 0], (2, 0, 1)).reshape(toks, narrow, 2, N2)
    last = jnp.zeros_like(first[0])
    for at in range(side):
        sent = jnp.where(tok == 0, first[side + at], first[at])
        last = last + lax.ppermute(sent, "tok", [(side, at), (0, side + at)])
    last = jnp.pad(last[:, :, None], ((0, 0), (0, 0), (0, ROWS - HALF - 1), (0, 0)))
    return jnp.concatenate([both, last], axis=2)


def shards(value, gate_in, gate_out, filter_spectrum, skip_gain):
    f32 = jnp.float32
    toks, segs = lax.axis_size("tok"), lax.axis_size("seg")
    narrow = value.shape[1] // toks
    step = narrow // CHUNKS
    base = lax.axis_index("tok") // (toks // 2) * HALF
    turned = turn_call(value, gate_in, toks)
    turned, filter_spectrum, base = lax.optimization_barrier((turned, filter_spectrum, base))
    tables = half_tables(base)
    filt = half_filter(filter_spectrum, narrow)
    onward = [(i, i + 1) for i in range(segs - 1)]
    pieces = []
    for at in range(CHUNKS):
        x = lax.all_to_all(turned[at], "tok", 0, 0, tiled=True)
        main, tail = conv_call(x, filt[at * step : (at + 1) * step], tables)
        carried = lax.ppermute(tail, "seg", onward)
        mixed = (main.astype(f32) + carried.astype(f32)).astype(jnp.bfloat16)
        pieces.append(lax.all_to_all(mixed, "tok", 0, 0, tiled=True))
    return finish_call(value, gate_in, gate_out, skip_gain, pieces)


def solution(mesh):
    return jax.shard_map(
        shards,
        mesh=mesh,
        in_specs=(
            P(("seg", "tok"), None),
            P(("seg", "tok"), None),
            P(("seg", "tok"), None),
            P(None, "tok", None, None),
            P(),
        ),
        out_specs=P(("seg", "tok"), None),
        check_vma=False,
    )
```

time: 312 us -> 321 us (1.029)
  local copies, waits for them, and re-layouts: 44.3 us -> 64.9 us
  other arithmetic: 54.3 us -> 35.4 us
  blocking collectives: 70 us -> 53.5 us
  Pallas kernels: 51.3 us -> 62.4 us
  waiting for transfers between devices: 54.5 us -> 63 us
  starting transfers between devices: 23.1 us -> 26.4 us
    optimization_barrier x0 -> x2, local copies, waits for them, and re-layouts: none -> 45.8 us  [shards(): lax.optimization_barrier((turned, filter_spectrum, base))]
    convert_element_type x3 -> x0, other arithmetic: 19.5 us -> none  [the longest x1 8.72 us: shards(): return result.astype(jnp.bfloat16)]
    all_to_all x1 -> x0, blocking collectives: 17.2 us -> none  [half_filter(): lax.all_to_all(mine, 'tok', 0, 0, axis_index_groups=groups, tiled=True)]
    ppermute x0 -> x3, waiting for transfers between devices: none -> 12.1 us  [the longest x1 12.1 us: half_filter(): part = lax.ppermute(part, 'tok', pairs)]
    pallas_call x2 -> x4, Pallas kernels: 51.3 us -> 62.4 us  [the longest x2 39 us: conv_call(): pl.pallas_call(conv_kernel, grid=(count // group,), in_specs=[block, pl.B...]
    convert_element_type x1 -> x0, local copies, waits for them, and re-layouts: 10 us -> none  [shards(): mixed.astype(f32) + skip_gain[None, :] * gated.astype(f32)]
    reshape x2 -> x0, local copies, waits for them, and re-layouts: 8.64 us -> none  [the longest x1 7.89 us: shards(): turned = jnp.transpose(gated.reshape(rows, N2, channels), (2, 0, 1))]
    ppermute x0 -> x3, starting transfers between devices: none -> 8.19 us  [the longest x2 6.55 us: half_filter(): last = last + lax.ppermute(sent, 'tok', [(side, at), (0, side + at)])]
  transfers between devices with their start and end apart: 7 -> 9, of which waited for: 3 -> 3; matrix products, arithmetic and copies ran while one was open for 22% -> 23% of each run, Pallas kernels for 16% -> 12%
where the time goes in v2:
time: 321 us; the launch traced here: 319 us
  local copies, waits for them, and re-layouts  64.9 us (20%)
  waiting for transfers between devices  63 us (20%)
  Pallas kernels  62.4 us (19%)
  blocking collectives  53.5 us (17%)
  other arithmetic  35.4 us (11%)
  starting transfers between devices  26.4 us (8%)
  between operations  13.6 us (4%)
    all_to_all x1, blocking collectives, shards(): pieces.append(lax.all_to_all(mixed, 'tok', 0, 0, tiled=True))  53.5 us
    ppermute x2, waiting for transfers between devices, shards(): carried = lax.ppermute(tail, 'seg', onward)  50.8 us
    optimization_barrier x2, local copies, waits for them, and re-layouts, shards(): lax.optimization_barrier((turned, filter_spectrum, base))  45.8 us
    pallas_call x2, Pallas kernels, conv_call(): pl.pallas_call(conv_kernel, grid=(count // group,), in_specs=[block, pl.B...  39 us
    ppermute x1, waiting for transfers between devices, half_filter(): part = lax.ppermute(part, 'tok', pairs)  12.1 us
    pallas_call x1, Pallas kernels, turn_call(): pl.pallas_call(turn_kernel, grid=(rows // lines,), in_specs=[flat, flat],...  12 us
    pallas_call x1, Pallas kernels, finish_call(): pl.pallas_call(finish_kernel, grid=(rows // lines,), in_specs=[flat] * 3...  11.4 us
    concatenate x1, other arithmetic, half_tables(): back = jnp.block([[cos_two, sin_two], [-sin_two, cos_two]])  10.1 us
  transfers between devices with their start and end apart: 9, of which 3 were waited for; matrix products, arithmetic and copies ran while one was open for 23% of the time, Pallas kernels for 12%

profile of v2, /device:TPU:2, one launch (start us, length us, event | category | flops | bytes accessed | tf_op | source)
XLA Modules:
  0.0 319.1 jit_solution(18248055756936952429)
XLA Ops:
  6.5 12.0 %shard_map.55 = (bf16[4,16,32,512]{3,2,1,0:T(8,128)(2,1)}, bf16[4,16,32,512]{3,2,1,0:T(8,128)(2,1)}) custom-call(bf16[16384,128]{1,0:T(8,128)(2,1)} %value_ref.3, bf16[16384,128]{1,0:T(8,128)(2,1)} %gate_ref.3), custom_call_target="tpu_custom_call" | custom-call | flops 2097152 | bytes 12582912 | tf_op jit(solution)/shard_map/pallas_call | solution.py:69
  18.6 23.3 %copy.15 = bf16[2,64,512,128]{2,1,0,3:T(8,128)(2,1)} copy(bf16[2,64,512,128]{3,2,1,0:T(8,128)(2,1)} %param.8) | data formatting | bytes 33554432 | tf_op jit(solution)/shard_map/optimization_barrier | solution.py:216
  41.8 1.3 constant_dynamic-slice_fusion.1
  43.2 1.6 collective-permute-start
  44.8 12.1 %collective-permute-done = bf16[32,2,8,512]{3,2,1,0:T(8,128)(2,1)S(1)} collective-permute-done((bf16[32,2,8,512]{3,2,1,0:T(8,128)(2,1)S(1)}, bf16[32,2,8,512]{3,2,1,0:T(8,128)(2,1)S(1)}, u32[]{:S(2)}, u32[]{:S(2)}) %collective-permute-start) | collective-permute-done | bytes 524320 | tf_op jit(solution)/shard_map/ppermute | solution.py:192
  57.0 1.3 reverse_select_fusion
  58.3 4.9 %all-to-all-start = ((bf16[4,16,32,512]{3,2,1,0:T(8,128)(2,1)}), bf16[4,16,32,512]{3,2,1,0:T(8,128)(2,1)S(1)}, u32[]{:S(2)}, u32[]{:S(2)}) async-start(bf16[4,16,32,512]{3,2,1,0:T(8,128)(2,1)} %get-tuple-element.17), calls=%async_computation | async-start | bytes 4194304 | tf_op jit(solution)/shard_map/all_to_all | solution.py:222
  63.2 22.5 %copy.17 = bf16[2,64,512,128]{2,3,0,1:T(8,128)(2,1)} copy(bf16[2,64,512,128]{3,2,1,0:T(8,128)(2,1)} %param.8) | data formatting | bytes 33554432 | tf_op jit(solution)/shard_map/optimization_barrier | solution.py:216
  85.8 1.0 slice_bitcast_fusion
  86.8 4.8 %collective-permute-start.1 = (bf16[32,2,512]{2,0,1:T(8,128)(2,1)S(1)}, bf16[32,2,512]{2,0,1:T(8,128)(2,1)S(1)}, u32[]{:S(2)}, u32[]{:S(2)}) collective-permute-start(bf16[32,2,512]{2,0,1:T(8,128)(2,1)S(1)} %get-tuple-element.34), channel_id=1, source_target_pairs={{2,0},{0,2},{6,4},{4,6},{10,8},{8,10},{14,12},{12,14},{18,16},{16,... | collective-permute-start | bytes 196616 | tf_op jit(solution)/shard_map/ppermute | solution.py:204
  91.6 1.7 collective-permute-start.2
  93.6 1.0 multiply_convert_fusion
  94.8 4.0 %fusion.16 = bf16[512,512]{1,0:T(8,128)(2,1)S(1)} fusion(), kind=kLoop, calls=%fused_computation.43 | loop fusion | flops 4718592 | bytes 524288 | tf_op jit(solution)/shard_map/neg | solution.py:41
  98.8 1.2 fusion.22
  100.0 4.3 %sine_convert_fusion = (bf16[512,512]{1,0:T(8,128)(2,1)S(1)}, bf16[512,512]{1,0:T(8,128)(2,1)S(1)}) fusion(), kind=kLoop, calls=%fused_computation.19 | loop fusion | flops 4194304 | bytes 1048576 | tf_op jit(solution)/shard_map/convert_element_type | solution.py:40
  104.4 0.4 cosine_convert_fusion.2
  104.7 10.1 %fusion.3 = (bf16[1024,1024]{1,0:T(8,128)(2,1)}, bf16[1024,1024]{1,0:T(8,128)(2,1)}) fusion(bf16[512,512]{1,0:T(8,128)(2,1)S(1)} %get-tuple-element.40, bf16[512,512]{1,0:T(8,128)(2,1)S(1)} %fusion.16, bf16[512,512]{1,0:T(8,128)(2,1)S(1)} %get-tuple-element.39), kind=kLoop, calls=%fused_computation.10 | loop fusion | flops 14680064 | bytes 5767168 | tf_op jit(solution)/shard_map/jit(block)/concatenate | solution.py:42
  115.0 8.0 %copy.16 = bf16[32,2,2,8,8,512]{5,4,3,2,1,0:T(8,128)(2,1)} copy(bf16[32,2,2,8,8,512]{5,4,1,0,2,3:T(8,128)(2,1)} %bitcast.19) | data formatting | bytes 16777216 | tf_op jit(solution)/shard_map/transpose | solution.py:199
  122.9 8.2 %fusion.1 = bf16[32,2,144,512]{3,2,1,0:T(8,128)(2,1)} fusion(bf16[32,2,1,512]{3,2,1,0:T(2,128)(2,1)S(1)} %copy.18, bf16[32,2,128,512]{3,2,1,0:T(8,128)(2,1)} %bitcast.18), kind=kLoop, calls=%fused_computation.2 | loop fusion | flops 28311552 | bytes 17891328 | tf_op jit(solution)/shard_map/concatenate | solution.py:206
  131.1 8.6 %fusion.35 = (bf16[16,2,144,512]{3,2,1,0:T(8,128)(2,1)}, bf16[16,2,144,512]{3,2,1,0:T(8,128)(2,1)}) fusion(bf16[32,2,144,512]{3,2,1,0:T(8,128)(2,1)} %fusion.1), kind=kLoop, calls=%fused_computation.80 | loop fusion | bytes 18874368 | tf_op jit(solution)/shard_map/slice | solution.py:223
  139.7 4.7 %all-to-all-start.2 = ((bf16[4,16,32,512]{3,2,1,0:T(8,128)(2,1)}), bf16[4,16,32,512]{3,2,1,0:T(8,128)(2,1)}, u32[]{:S(2)}, u32[]{:S(2)}) async-start(bf16[4,16,32,512]{3,2,1,0:T(8,128)(2,1)} %get-tuple-element.22), calls=%async_computation.2 | async-start | bytes 4194304 | tf_op jit(solution)/shard_map/all_to_all | solution.py:222
  144.4 19.5 %shard_map.56 = (bf16[4,16,32,512]{3,2,1,0:T(8,128)(2,1)S(1)}, bf16[4,16,32,512]{3,2,1,0:T(8,128)(2,1)S(1)}) custom-call(bf16[4,16,32,512]{3,2,1,0:T(8,128)(2,1)} %copy-done.1, bf16[16,2,144,512]{3,2,1,0:T(8,128)(2,1)} %get-tuple-element.26.h_ref, bf16[288,128]{1,0:T(8,128)(2,1)S(1)} %pad_maximum_fusion.7.fwd_ref, ...), custom_call_target="tpu_custom_call" | custom-call | flops 11475615744 | bytes 11010048 | tf_op jit(solution)/shard_map/pallas_call | solution.py:160
  163.9 1.9 collective-permute-start.3
  165.8 25.4 %collective-permute-done.3 = bf16[4,16,32,512]{3,2,1,0:T(8,128)(2,1)S(1)} collective-permute-done((bf16[4,16,32,512]{3,2,1,0:T(8,128)(2,1)S(1)}, bf16[4,16,32,512]{3,2,1,0:T(8,128)(2,1)S(1)}, u32[]{:S(2)}, u32[]{:S(2)}) %collective-permute-start.3) | collective-permute-done | bytes 2097184 | tf_op jit(solution)/shard_map/ppermute | solution.py:224
  191.3 2.2 add_convert_fusion.1
  193.5 4.8 %all-to-all-start.1 = ((bf16[4,16,32,512]{3,2,1,0:T(8,128)(2,1)}), bf16[4,16,32,512]{3,2,1,0:T(8,128)(2,1)S(1)}, u32[]{:S(2)}, u32[]{:S(2)}) async-start(bf16[4,16,32,512]{3,2,1,0:T(8,128)(2,1)} %add_convert_fusion.1), calls=%async_computation.1 | async-start | bytes 4194304 | tf_op jit(solution)/shard_map/all_to_all | solution.py:226
  198.3 19.5 %shard_map.57 = (bf16[4,16,32,512]{3,2,1,0:T(8,128)(2,1)S(1)}, bf16[4,16,32,512]{3,2,1,0:T(8,128)(2,1)S(1)}) custom-call(bf16[4,16,32,512]{3,2,1,0:T(8,128)(2,1)} %all-to-all-done.2.x_ref, bf16[16,2,144,512]{3,2,1,0:T(8,128)(2,1)} %get-tuple-element.25.h_ref, bf16[288,128]{1,0:T(8,128)(2,1)S(1)} %pad_maximum_fusion.7.fwd_ref, ...), custom_call_target="tpu_custom_call" | custom-call | flops 11475615744 | bytes 11010048 | tf_op jit(solution)/shard_map/pallas_call | solution.py:160
  217.8 1.9 collective-permute-start.4
  219.7 25.4 %collective-permute-done.4 = bf16[4,16,32,512]{3,2,1,0:T(8,128)(2,1)S(1)} collective-permute-done((bf16[4,16,32,512]{3,2,1,0:T(8,128)(2,1)S(1)}, bf16[4,16,32,512]{3,2,1,0:T(8,128)(2,1)S(1)}, u32[]{:S(2)}, u32[]{:S(2)}) %collective-permute-start.4) | collective-permute-done | bytes 2097184 | tf_op jit(solution)/shard_map/ppermute | solution.py:224
  245.2 2.3 add_convert_fusion
  247.4 53.5 %all_to_all.20.refs_1_ = bf16[4,16,32,512]{3,2,1,0:T(8,128)(2,1)S(1)} all-to-all(bf16[4,16,32,512]{3,2,1,0:T(8,128)(2,1)} %add_convert_fusion), channel_id=1, replica_groups=mesh['seg'=8,'tok'=4] {'tok'}, dimensions={0} | all-to-all | bytes 4194304 | tf_op jit(solution)/shard_map/all_to_all | solution.py:226
  300.9 11.4 %shard_map.58 = bf16[16384,128]{1,0:T(8,128)(2,1)} custom-call(bf16[16384,128]{1,0:T(8,128)(2,1)} %value_ref.3, bf16[16384,128]{1,0:T(8,128)(2,1)} %gate_ref.3, bf16[16384,128]{1,0:T(8,128)(2,1)} %gate_out_ref.1, f32[1,128]{1,0:T(1,128)S(1)} %bitcast.17, bf16[4,16,32,512]{3,2,1,0:T(8,128)(2,1)S(1)} %all-to-all-done.1.refs_0_, ...), custom_call_target="tpu_custom_call" | custom-call | flops 8388608 | bytes 20971520 | tf_op jit(solution)/shard_map/pallas_call | solution.py:104
  (24 shorter events, 0.8 us)
Async XLA Ops:
  6.5 108.4 %all-gather.3.cloned.1.call-start = ((), (), s32[]{:S(2)}) async-start(), calls=%async_computation.4 | async-start | bytes 9437184 | tf_op jit(solution)/shard_map/all_gather | solution.py:198
  43.2 13.7 %collective-permute-start = (bf16[32,2,8,512]{3,2,1,0:T(8,128)(2,1)S(1)}, bf16[32,2,8,512]{3,2,1,0:T(8,128)(2,1)S(1)}, u32[]{:S(2)}, u32[]{:S(2)}) collective-permute-start(bf16[32,2,8,512]{3,2,1,0:T(8,128)(2,1)S(1)} %get-tuple-element.30), channel_id=1, source_target_pairs={{0,1},{1,0},{2,3},{3,2},{4,5},{5,4},{6,7},{7,6},{8,9},{9,8},{10,11... | collective-permute-start | bytes 1572872 | tf_op jit(solution)/shard_map/ppermute | solution.py:192
  58.3 81.4 %all-to-all-start = ((bf16[4,16,32,512]{3,2,1,0:T(8,128)(2,1)}), bf16[4,16,32,512]{3,2,1,0:T(8,128)(2,1)S(1)}, u32[]{:S(2)}, u32[]{:S(2)}) async-start(bf16[4,16,32,512]{3,2,1,0:T(8,128)(2,1)} %get-tuple-element.17), calls=%async_computation | async-start | bytes 4194304 | tf_op jit(solution)/shard_map/all_to_all | solution.py:222
  86.8 28.1 %collective-permute-start.1 = (bf16[32,2,512]{2,0,1:T(8,128)(2,1)S(1)}, bf16[32,2,512]{2,0,1:T(8,128)(2,1)S(1)}, u32[]{:S(2)}, u32[]{:S(2)}) collective-permute-start(bf16[32,2,512]{2,0,1:T(8,128)(2,1)S(1)} %get-tuple-element.34), channel_id=1, source_target_pairs={{2,0},{0,2},{6,4},{4,6},{10,8},{8,10},{14,12},{12,14},{18,16},{16,... | collective-permute-start | bytes 196616 | tf_op jit(solution)/shard_map/ppermute | solution.py:204
  91.6 23.3 %collective-permute-start.2 = (bf16[32,2,512]{2,0,1:T(8,128)(2,1)S(1)}, bf16[32,2,512]{2,0,1:T(8,128)(2,1)S(1)}, u32[]{:S(2)}, u32[]{:S(2)}) collective-permute-start(bf16[32,2,512]{2,0,1:T(8,128)(2,1)S(1)} %get-tuple-element.33), channel_id=1, source_target_pairs={{2,1},{0,3},{6,5},{4,7},{10,9},{8,11},{14,13},{12,15},{18,17},{16,... | collective-permute-start | bytes 196616 | tf_op jit(solution)/shard_map/ppermute | solution.py:204
  139.7 4.7 %copy-start.1 = (bf16[4,16,32,512]{3,2,1,0:T(8,128)(2,1)}, bf16[4,16,32,512]{3,2,1,0:T(8,128)(2,1)S(1)}, u32[]{:S(2)}) copy-start(bf16[4,16,32,512]{3,2,1,0:T(8,128)(2,1)S(1)} %all-to-all-done.x_ref) | copy-start | bytes 6291460
  139.7 53.8 %all-to-all-start.2 = ((bf16[4,16,32,512]{3,2,1,0:T(8,128)(2,1)}), bf16[4,16,32,512]{3,2,1,0:T(8,128)(2,1)}, u32[]{:S(2)}, u32[]{:S(2)}) async-start(bf16[4,16,32,512]{3,2,1,0:T(8,128)(2,1)} %get-tuple-element.22), calls=%async_computation.2 | async-start | bytes 4194304 | tf_op jit(solution)/shard_map/all_to_all | solution.py:222
  163.9 27.4 %collective-permute-start.3 = (bf16[4,16,32,512]{3,2,1,0:T(8,128)(2,1)S(1)}, bf16[4,16,32,512]{3,2,1,0:T(8,128)(2,1)S(1)}, u32[]{:S(2)}, u32[]{:S(2)}) collective-permute-start(bf16[4,16,32,512]{3,2,1,0:T(8,128)(2,1)S(1)} %get-tuple-element.21), channel_id=1, source_target_pairs={{0,4},{4,8},{8,12},{12,16},{16,20},{20,24},{24,28},{1,5},{5,9},{9,... | collective-permute-start | bytes 6291464 | tf_op jit(solution)/shard_map/ppermute | solution.py:224
  193.5 53.9 %all-to-all-start.1 = ((bf16[4,16,32,512]{3,2,1,0:T(8,128)(2,1)}), bf16[4,16,32,512]{3,2,1,0:T(8,128)(2,1)S(1)}, u32[]{:S(2)}, u32[]{:S(2)}) async-start(bf16[4,16,32,512]{3,2,1,0:T(8,128)(2,1)} %add_convert_fusion.1), calls=%async_computation.1 | async-start | bytes 4194304 | tf_op jit(solution)/shard_map/all_to_all | solution.py:226
  217.8 27.4 %collective-permute-start.4 = (bf16[4,16,32,512]{3,2,1,0:T(8,128)(2,1)S(1)}, bf16[4,16,32,512]{3,2,1,0:T(8,128)(2,1)S(1)}, u32[]{:S(2)}, u32[]{:S(2)}) collective-permute-start(bf16[4,16,32,512]{3,2,1,0:T(8,128)(2,1)S(1)} %get-tuple-element.24), channel_id=1, source_target_pairs={{0,4},{4,8},{8,12},{12,16},{16,20},{20,24},{24,28},{1,5},{5,9},{9,... | collective-permute-start | bytes 6291464 | tf_op jit(solution)/shard_map/ppermute | solution.py:224
  245.2 55.7 %copy-start = (f32[128]{0:T(128)S(1)}, f32[128]{0:T(128)}, u32[]{:S(2)}) copy-start(f32[128]{0:T(128)} %param.9) | copy-start | bytes 1540
Sparse Core Ops, SparseCore 0:
  58.5 55.6 all-gather.2

commit v3 on v2

--- a/solution.py
+++ b/solution.py
@@ -2,6 +2,7 @@
 
 import jax
 import jax.numpy as jnp
+import numpy as np
 from jax import lax
 from jax.experimental import pallas as pl
 from jax.experimental.pallas import tpu as pltpu
@@ -16,34 +17,38 @@
 GROUP = 4
 
 
-def span_ids(count):
-    return jnp.arange(count, dtype=jnp.int32)
-
-
 def trig_tables(row_ids, col_ids, modulus):
     product = row_ids[:, None] * col_ids[None, :] % modulus
-    angle = product.astype(jnp.float32) * jnp.float32(2.0 * math.pi / modulus)
-    return (jnp.cos(angle), jnp.sin(angle))
-
-
-def half_tables(base):
-    rows = span_ids(ROWS)
-    k1 = (base + rows) % N1
-    used = rows <= HALF
-    weight = jnp.where(used, jnp.where((rows == 0) | (rows == HALF), 1.0, 2.0), 0.0)
-    weight = weight.astype(jnp.float32) / (N1 * N2)
-    cos_one, sin_one = trig_tables(k1, span_ids(HALF), N1)
-    forward = jnp.concatenate([cos_one, -sin_one], axis=0).astype(jnp.bfloat16)
-    tw = jnp.stack(trig_tables(k1, span_ids(N2), N1 * N2))
-    cos_two, sin_two = trig_tables(span_ids(N2), span_ids(N2), N2)
-    cos_two = cos_two.astype(jnp.bfloat16)
-    sin_two = sin_two.astype(jnp.bfloat16)
-    there = jnp.block([[cos_two, -sin_two], [sin_two, cos_two]])
-    back = jnp.block([[cos_two, sin_two], [-sin_two, cos_two]])
-    inv_cos, inv_sin = trig_tables(span_ids(N1), k1, N1)
-    inv_cos = inv_cos.astype(jnp.bfloat16).astype(jnp.float32) * weight[None, :]
-    inv_sin = inv_sin.astype(jnp.bfloat16).astype(jnp.float32) * weight[None, :]
-    inverse = jnp.concatenate([inv_cos, -inv_sin], axis=1).astype(jnp.bfloat16)
+    angle = product.astype(np.float32) * np.float32(2.0 * math.pi / modulus)
+    return (np.cos(angle), np.sin(angle))
+
+
+def rounded(table):
+    return table.astype(jnp.bfloat16)
+
+
+def row_tables(base, order):
+    order = np.concatenate([order, np.zeros(ROWS - len(order), np.int32)])
+    k1 = (base + order) % N1
+    weight = np.where((order == 0) | (order == HALF), 1.0, 2.0)
+    weight[HALF + 1 :] = 0.0
+    weight = weight.astype(np.float32) / np.float32(N1 * N2)
+    cos_one, sin_one = trig_tables(k1, np.arange(HALF, dtype=np.int32), N1)
+    forward = rounded(np.concatenate([cos_one, -sin_one], axis=0))
+    tw = np.stack(trig_tables(k1, np.arange(N2, dtype=np.int32), N1 * N2))
+    inv = trig_tables(np.arange(N1, dtype=np.int32), k1, N1)
+    inv_cos, inv_sin = [rounded(t).astype(np.float32) * weight[None, :] for t in inv]
+    inverse = rounded(np.concatenate([inv_cos, -inv_sin], axis=1))
+    return forward, tw, inverse
+
+
+def half_tables(upper, order):
+    halves = zip(row_tables(0, order), row_tables(HALF, order))
+    forward, tw, inverse = [jnp.where(upper == 0, *pair) for pair in halves]
+    cos_two, sin_two = trig_tables(*[np.arange(N2, dtype=np.int32)] * 2, N2)
+    cos_two, sin_two = rounded(cos_two), rounded(sin_two)
+    there = jnp.asarray(np.block([[cos_two, -sin_two], [sin_two, cos_two]]))
+    back = jnp.asarray(np.block([[cos_two, sin_two], [-sin_two, cos_two]]))
     return forward, tw, there, back, inverse
 
 
@@ -114,7 +119,7 @@
     )(value, gate, gate_out, skip[None, :], *pieces)
 
 
-def conv_kernel(x_ref, h_ref, fwd_ref, tw_ref, there_ref, back_ref, inv_ref, main_ref, tail_ref):
+def conv_kernel(x_ref, h_ref, last_ref, fwd_ref, tw_ref, there_ref, back_ref, inv_ref, main_ref, tail_ref):
     f32 = jnp.float32
     toks, count, rows, _ = x_ref.shape
     tc, ts = tw_ref[0], tw_ref[1]
@@ -132,8 +137,11 @@
     for i in range(count):
         part = spec[i * ROWS : (i + 1) * ROWS]
         s_re, s_im = part[:, :N2], part[:, N2:]
-        h_re = h_ref[i, 0].astype(f32)
-        h_im = h_ref[i, 1].astype(f32)
+        h = h_ref[:, :, i].astype(f32)
+        share = h.shape[2] // 2
+        last = last_ref[i].astype(f32)
+        h_re = jnp.concatenate([h[:, :, :share].reshape(HALF, N2), last[:16]], axis=0)
+        h_im = jnp.concatenate([h[:, :, share:].reshape(HALF, N2), last[16:]], axis=0)
         z_re = (s_re * h_re - s_im * h_im).astype(jnp.bfloat16)
         z_im = (s_re * h_im + s_im * h_re).astype(jnp.bfloat16)
         z.append(jnp.concatenate([z_re, z_im], axis=1))
@@ -150,9 +158,10 @@
         tail_ref[:, i] = conv[HALF:].reshape(toks, rows, N2).astype(jnp.bfloat16)
 
 
-def conv_call(x, h, tables):
+def conv_call(x, h, last, at, tables):
     parts, count, rows, _ = x.shape
     group = min(count, GROUP)
+    first = at * (count // group)
     block = pl.BlockSpec((parts, group, rows, N2), lambda c: (0, c, 0, 0))
     whole = lambda t: pl.BlockSpec(t.shape, lambda c: (0,) * t.ndim)
     out = jax.ShapeDtypeStruct(x.shape, jnp.bfloat16)
@@ -160,30 +169,33 @@
     return pl.pallas_call(
         conv_kernel,
         grid=(count // group,),
-        in_specs=[block, pl.BlockSpec((group, 2, ROWS, N2), lambda c: (c, 0, 0, 0))]
+        in_specs=[
+            block,
+            pl.BlockSpec(h.shape[:2] + (group,) + h.shape[3:], lambda c: (0, 0, c + first, 0, 0)),
+            pl.BlockSpec((group,) + last.shape[1:], lambda c: (c + first, 0, 0)),
+        ]
         + [whole(t) for t in tables],
         out_specs=[block, block],
         out_shape=[out, out],
         compiler_params=pltpu.CompilerParams(vmem_limit_bytes=48 * 1024 * 1024),
         cost_estimate=pl.CostEstimate(
-            flops=flops, bytes_accessed=6 * x.size + 2 * h.size, transcendentals=0
-        ),
-    )(x, h, *tables)
+            flops=flops, bytes_accessed=6 * x.size + 2 * h.size // CHUNKS, transcendentals=0
+        ),
+    )(x, h, last, *tables)
 
 
 def half_filter(filt, narrow):
     toks, segs = lax.axis_size("tok"), lax.axis_size("seg")
     tok, seg = lax.axis_index("tok"), lax.axis_index("seg")
-    rows = filt.shape[1]
-    channels = filt.shape[3]
+    rows, channels = filt.shape[1], filt.shape[3]
     share = rows // segs
     side = toks // 2
     upper = tok // side
+    own = tok % side
     mine = lax.dynamic_slice(
         filt, (0, seg * share, 0, upper * (channels // 2)), (2, share, N2, channels // 2)
     )
-    mine = jnp.transpose(mine, (3, 0, 1, 2)).reshape(side, narrow, 2, share, N2)
-    own = tok % side
+    mine = jnp.transpose(mine, (3, 0, 1, 2)).reshape(side, narrow, 2 * share, N2)
     parts = []
     for by in range(side):
         part = lax.dynamic_index_in_dim(mine, (own + side - by) % side, 0, keepdims=False)
@@ -191,36 +203,39 @@
             pairs = [(t, t // side * side + (t + side - by) % side) for t in range(toks)]
             part = lax.ppermute(part, "tok", pairs)
         parts.append(part)
-    mine = jnp.stack(parts)
-    mine = jnp.take(mine, (span_ids(side) - own) % side, axis=0) if side > 2 else jnp.where(
-        own == 0, mine, mine[::-1]
-    )
+    if side == 2:
+        mine = jnp.where(own == 0, jnp.stack(parts), jnp.stack(parts[::-1]))
+    else:
+        mine = jnp.take(jnp.stack(parts), (jnp.arange(side) + side - own) % side, axis=0)
     both = lax.all_gather(mine, "seg")
-    both = jnp.transpose(both, (2, 3, 1, 0, 4, 5)).reshape(narrow, 2, HALF, N2)
+    order = np.arange(HALF, dtype=np.int32)
+    if share % 8:
+        both = both.reshape(segs, side, narrow, 2, share, N2)
+        both = jnp.transpose(both, (2, 3, 1, 0, 4, 5)).reshape(1, 1, narrow, 2 * HALF, N2)
+    else:
+        order = np.transpose(order.reshape(side, segs, share), (1, 0, 2)).reshape(HALF)
+    order = np.append(order, np.int32(HALF))
     first = jnp.transpose(filt[:, 0], (2, 0, 1)).reshape(toks, narrow, 2, N2)
     last = jnp.zeros_like(first[0])
     for at in range(side):
         sent = jnp.where(tok == 0, first[side + at], first[at])
         last = last + lax.ppermute(sent, "tok", [(side, at), (0, side + at)])
-    last = jnp.pad(last[:, :, None], ((0, 0), (0, 0), (0, ROWS - HALF - 1), (0, 0)))
-    return jnp.concatenate([both, last], axis=2)
+    last = jnp.pad(last[:, :, None], ((0, 0), (0, 0), (0, 15), (0, 0)))
+    return both, last.reshape(narrow, 32, N2), order
 
 
 def shards(value, gate_in, gate_out, filter_spectrum, skip_gain):
     f32 = jnp.float32
     toks, segs = lax.axis_size("tok"), lax.axis_size("seg")
     narrow = value.shape[1] // toks
-    step = narrow // CHUNKS
-    base = lax.axis_index("tok") // (toks // 2) * HALF
     turned = turn_call(value, gate_in, toks)
-    turned, filter_spectrum, base = lax.optimization_barrier((turned, filter_spectrum, base))
-    tables = half_tables(base)
-    filt = half_filter(filter_spectrum, narrow)
+    both, last, order = half_filter(filter_spectrum, narrow)
+    tables = half_tables(lax.axis_index("tok") // (toks // 2), order)
     onward = [(i, i + 1) for i in range(segs - 1)]
     pieces = []
     for at in range(CHUNKS):
         x = lax.all_to_all(turned[at], "tok", 0, 0, tiled=True)
-        main, tail = conv_call(x, filt[at * step : (at + 1) * step], tables)
+        main, tail = conv_call(x, both, last, at, tables)
         carried = lax.ppermute(tail, "seg", onward)
         mixed = (main.astype(f32) + carried.astype(f32)).astype(jnp.bfloat16)
         pieces.append(lax.all_to_all(mixed, "tok", 0, 0, tiled=True))

time: 321 us -> 281 us (0.88)
  local copies, waits for them, and re-layouts: 64.9 us -> 6.48 us
  waiting for transfers between devices: 63 us -> 109 us
  other arithmetic: 35.4 us -> 6.13 us
    ppermute x2, waiting for transfers between devices: 0.01 us -> 45.9 us  [half_filter(): last = last + lax.ppermute(sent, 'tok', [(side, at), (0, side + at)])]
    optimization_barrier x2 -> x0, local copies, waits for them, and re-layouts: 45.8 us -> none  [shards(): lax.optimization_barrier((turned, filter_spectrum, base))]
    concatenate x4 -> x0, other arithmetic: 18.4 us -> none  [the longest x1 10.1 us: half_tables(): back = jnp.block([[cos_two, sin_two], [-sin_two, cos_two]])]
    slice x1 -> x0, local copies, waits for them, and re-layouts: 8.57 us -> none  [shards(): main, tail = conv_call(x, filt[at * step:(at + 1) * step], tables)]
    transpose x1 -> x0, local copies, waits for them, and re-layouts: 7.96 us -> none  [half_filter(): both = jnp.transpose(both, (2, 3, 1, 0, 4, 5)).reshape(narrow, 2, HALF, N2)]
    convert_element_type x2 -> x0, other arithmetic: 4.44 us -> none  [the longest x1 4.31 us: half_tables(): sin_two = sin_two.astype(jnp.bfloat16)]
    neg x1 -> x0, other arithmetic: 4 us -> none  [half_tables(): there = jnp.block([[cos_two, -sin_two], [sin_two, cos_two]])]
  transfers between devices with their start and end apart: 9 -> 9, of which waited for: 3 -> 4; matrix products, arithmetic and copies ran while one was open for 23% -> 2% of each run, Pallas kernels for 12% -> 18%
where the time goes in v3:
time: 281 us
  waiting for transfers between devices  109 us (39%)
  Pallas kernels  63 us (22%)
  blocking collectives  53.6 us (19%)
  starting transfers between devices  29 us (10%)
  between operations  13.6 us (5%)
  local copies, waits for them, and re-layouts  6.48 us (2%)
  other arithmetic  6.13 us (2%)
    all_to_all x1, blocking collectives, shards(): pieces.append(lax.all_to_all(mixed, 'tok', 0, 0, tiled=True))  53.6 us
    ppermute x2, waiting for transfers between devices, shards(): carried = lax.ppermute(tail, 'seg', onward)  50.7 us
    ppermute x2, waiting for transfers between devices, half_filter(): last = last + lax.ppermute(sent, 'tok', [(side, at), (0, side + at)])  45.9 us
    pallas_call x2, Pallas kernels, conv_call(): pl.pallas_call(conv_kernel, grid=(count // group,), in_specs=[block, pl.B...  39.5 us
    pallas_call x1, Pallas kernels, turn_call(): pl.pallas_call(turn_kernel, grid=(rows // lines,), in_specs=[flat, flat],...  12.1 us
    ppermute x1, waiting for transfers between devices, half_filter(): part = lax.ppermute(part, 'tok', pairs)  12.1 us
    all_to_all x2, starting transfers between devices, shards(): x = lax.all_to_all(turned[at], 'tok', 0, 0, tiled=True)  11.8 us
    pallas_call x1, Pallas kernels, finish_call(): pl.pallas_call(finish_kernel, grid=(rows // lines,), in_specs=[flat] * 3...  11.4 us
  transfers between devices with their start and end apart: 9, of which 4 were waited for; matrix products, arithmetic and copies ran while one was open for 2% of the time, Pallas kernels for 18%

profile of v3, /device:TPU:2, one launch (start us, length us, event | category | flops | bytes accessed | tf_op | source)
XLA Modules:
  0.0 280.6 jit_solution(13849203332085353992)
XLA Ops:
  6.5 2.2 constant_dynamic-slice_fusion
  8.8 1.6 copy.21
  10.4 0.1 dynamic-slice_bitcast_fusion.1
  10.5 1.6 collective-permute-start
  12.1 12.1 %collective-permute-done = bf16[32,16,512]{2,1,0:T(8,128)(2,1)S(1)} collective-permute-done((bf16[32,16,512]{2,1,0:T(8,128)(2,1)S(1)}, bf16[32,16,512]{2,1,0:T(8,128)(2,1)S(1)}, u32[]{:S(2)}, u32[]{:S(2)}) %collective-permute-start) | collective-permute-done | bytes 524320 | tf_op jit(solution)/shard_map/ppermute | solution.py:204
  24.2 1.2 maximum_select_fusion
  25.4 0.0 all-gather.2.cloned.1.call-update
  25.4 12.1 %shard_map.127 = (bf16[4,16,32,512]{3,2,1,0:T(8,128)(2,1)}, bf16[4,16,32,512]{3,2,1,0:T(8,128)(2,1)}) custom-call(bf16[16384,128]{1,0:T(8,128)(2,1)} %value_ref.3, bf16[16384,128]{1,0:T(8,128)(2,1)} %gate_ref.3), custom_call_target="tpu_custom_call" | custom-call | flops 2097152 | bytes 12582912 | tf_op jit(solution)/shard_map/pallas_call | solution.py:74
  37.5 4.9 %all-to-all-start.2 = ((bf16[4,16,32,512]{3,2,1,0:T(8,128)(2,1)}), bf16[4,16,32,512]{3,2,1,0:T(8,128)(2,1)}, u32[]{:S(2)}, u32[]{:S(2)}) async-start(bf16[4,16,32,512]{3,2,1,0:T(8,128)(2,1)} %get-tuple-element.14), calls=%async_computation.2 | async-start | bytes 4194304 | tf_op jit(solution)/shard_map/all_to_all | solution.py:237
  42.4 0.0 copy-start.4
  42.4 1.1 slice_bitcast_fusion
  43.5 0.0 copy-start.7
  43.6 0.3 slice_select_fusion
  43.8 4.8 %collective-permute-start.1 = (bf16[32,2,512]{0,2,1:T(8,128)(2,1)S(1)}, bf16[32,2,512]{0,2,1:T(8,128)(2,1)S(1)}, u32[]{:S(2)}, u32[]{:S(2)}) collective-permute-start(bf16[32,2,512]{0,2,1:T(8,128)(2,1)S(1)} %get-tuple-element.20), channel_id=1, source_target_pairs={{2,0},{0,2},{6,4},{4,6},{10,8},{8,10},{14,12},{12,14},{18,16},{16,... | collective-permute-start | bytes 196616 | tf_op jit(solution)/shard_map/ppermute | solution.py:222
  48.7 1.6 collective-permute-start.2
  50.3 0.1 broadcast_select_fusion.tw_ref
  50.5 45.9 %collective-permute-done.1 = bf16[32,2,512]{0,2,1:T(8,128)(2,1)S(1)} collective-permute-done((bf16[32,2,512]{0,2,1:T(8,128)(2,1)S(1)}, bf16[32,2,512]{0,2,1:T(8,128)(2,1)S(1)}, u32[]{:S(2)}, u32[]{:S(2)}) %collective-permute-start.1) | collective-permute-done | bytes 65568 | tf_op jit(solution)/shard_map/ppermute | solution.py:222
  96.5 0.2 copy.22
  96.7 0.2 pad.4.clone
  96.9 6.9 %all-to-all-start = ((bf16[4,16,32,512]{3,2,1,0:T(8,128)(2,1)}), bf16[4,16,32,512]{3,2,1,0:T(8,128)(2,1)}, u32[]{:S(2)}, u32[]{:S(2)}) async-start(bf16[4,16,32,512]{3,2,1,0:T(8,128)(2,1)} %get-tuple-element.11), calls=%async_computation | async-start | bytes 4194304 | tf_op jit(solution)/shard_map/all_to_all | solution.py:237
  103.8 20.1 %shard_map.129 = (bf16[4,16,32,512]{3,2,1,0:T(8,128)(2,1)S(1)}, bf16[4,16,32,512]{3,2,1,0:T(8,128)(2,1)S(1)}) custom-call(bf16[4,16,32,512]{3,2,1,0:T(8,128)(2,1)} %all-to-all-done.2.x_ref, bf16[8,2,32,16,512]{4,3,2,1,0:T(8,128)(2,1)} %all-gather.2.cloned.1.call-done.h_ref, bf16[32,32,512]{2,1,0:T(8,128)(2,1)S(1)} %bitcast.16, ...), custom_call_target="tpu_custom_call" | custom-call | flops 11475615744 | bytes 10485760 | tf_op jit(solution)/shard_map/pallas_call | solution.py:169
  123.9 2.1 collective-permute-start.4
  126.0 25.2 %collective-permute-done.4 = bf16[4,16,32,512]{3,2,1,0:T(8,128)(2,1)S(1)} collective-permute-done((bf16[4,16,32,512]{3,2,1,0:T(8,128)(2,1)S(1)}, bf16[4,16,32,512]{3,2,1,0:T(8,128)(2,1)S(1)}, u32[]{:S(2)}, u32[]{:S(2)}) %collective-permute-start.4) | collective-permute-done | bytes 2097184 | tf_op jit(solution)/shard_map/ppermute | solution.py:239
  151.3 2.3 add_convert_fusion
  153.5 5.1 %all-to-all-start.3 = ((bf16[4,16,32,512]{3,2,1,0:T(8,128)(2,1)}), bf16[4,16,32,512]{3,2,1,0:T(8,128)(2,1)S(1)}, u32[]{:S(2)}, u32[]{:S(2)}) async-start(bf16[4,16,32,512]{3,2,1,0:T(8,128)(2,1)} %add_convert_fusion), calls=%async_computation.3 | async-start | bytes 4194304 | tf_op jit(solution)/shard_map/all_to_all | solution.py:241
  158.6 1.1 copy-done.1
  159.7 19.4 %shard_map.128 = (bf16[4,16,32,512]{3,2,1,0:T(8,128)(2,1)S(1)}, bf16[4,16,32,512]{3,2,1,0:T(8,128)(2,1)S(1)}) custom-call(bf16[4,16,32,512]{3,2,1,0:T(8,128)(2,1)} %all-to-all-done.x_ref, bf16[8,2,32,16,512]{4,3,2,1,0:T(8,128)(2,1)} %all-gather.2.cloned.1.call-done.h_ref, bf16[32,32,512]{2,1,0:T(8,128)(2,1)S(1)} %bitcast.17, ...), custom_call_target="tpu_custom_call" | custom-call | flops 11475615744 | bytes 10485760 | tf_op jit(solution)/shard_map/pallas_call | solution.py:169
  179.1 1.9 collective-permute-start.3
  181.1 25.4 %collective-permute-done.3 = bf16[4,16,32,512]{3,2,1,0:T(8,128)(2,1)S(1)} collective-permute-done((bf16[4,16,32,512]{3,2,1,0:T(8,128)(2,1)S(1)}, bf16[4,16,32,512]{3,2,1,0:T(8,128)(2,1)S(1)}, u32[]{:S(2)}, u32[]{:S(2)}) %collective-permute-start.3) | collective-permute-done | bytes 2097184 | tf_op jit(solution)/shard_map/ppermute | solution.py:239
  206.5 2.2 add_convert_fusion.1
  208.7 53.6 %all_to_all.20.refs_0_ = bf16[4,16,32,512]{3,2,1,0:T(8,128)(2,1)S(1)} all-to-all(bf16[4,16,32,512]{3,2,1,0:T(8,128)(2,1)} %add_convert_fusion.1), channel_id=1, replica_groups=mesh['seg'=8,'tok'=4] {'tok'}, dimensions={0} | all-to-all | bytes 4194304 | tf_op jit(solution)/shard_map/all_to_all | solution.py:241
  262.4 11.4 %shard_map.130 = bf16[16384,128]{1,0:T(8,128)(2,1)} custom-call(bf16[16384,128]{1,0:T(8,128)(2,1)} %value_ref.3, bf16[16384,128]{1,0:T(8,128)(2,1)} %gate_ref.3, bf16[16384,128]{1,0:T(8,128)(2,1)} %gate_out_ref.1, f32[1,128]{1,0:T(1,128)S(1)} %bitcast.18, bf16[4,16,32,512]{3,2,1,0:T(8,128)(2,1)S(1)} %all_to_all.20.refs_0_, ...), custom_call_target="tpu_custom_call" | custom-call | flops 8388608 | bytes 20971520 | tf_op jit(solution)/shard_map/pallas_call | solution.py:109
  (24 shorter events, 0.1 us)
Async XLA Ops:
  6.5 97.3 %all-gather.2.cloned.1.call-start = ((), (), s32[]{:S(2)}) async-start(), calls=%async_computation.4 | async-start | bytes 9437184 | tf_op jit(solution)/shard_map/all_gather | solution.py:210
  10.5 13.7 %collective-permute-start = (bf16[32,16,512]{2,1,0:T(8,128)(2,1)S(1)}, bf16[32,16,512]{2,1,0:T(8,128)(2,1)S(1)}, u32[]{:S(2)}, u32[]{:S(2)}) collective-permute-start(bf16[32,16,512]{2,1,0:T(8,128)(2,1)S(1)} %get-tuple-element.18), channel_id=1, source_target_pairs={{0,1},{1,0},{2,3},{3,2},{4,5},{5,4},{6,7},{7,6},{8,9},{9,8},{10,11... | collective-permute-start | bytes 1572872 | tf_op jit(solution)/shard_map/ppermute | solution.py:204
  37.5 59.3 %all-to-all-start.2 = ((bf16[4,16,32,512]{3,2,1,0:T(8,128)(2,1)}), bf16[4,16,32,512]{3,2,1,0:T(8,128)(2,1)}, u32[]{:S(2)}, u32[]{:S(2)}) async-start(bf16[4,16,32,512]{3,2,1,0:T(8,128)(2,1)} %get-tuple-element.14), calls=%async_computation.2 | async-start | bytes 4194304 | tf_op jit(solution)/shard_map/all_to_all | solution.py:237
  42.4 7.9 %copy-start.5 = (bf16[256,288]{1,0:T(8,128)(2,1)S(1)}, bf16[256,288]{1,0:T(8,128)(2,1)}, u32[]{:S(2)}) copy-start(bf16[256,288]{1,0:T(8,128)(2,1)} %constant.81.clone) | copy-start | bytes 442372
  42.4 7.9 %copy-start.6 = (bf16[256,288]{1,0:T(8,128)(2,1)S(1)}, bf16[256,288]{1,0:T(8,128)(2,1)}, u32[]{:S(2)}) copy-start(bf16[256,288]{1,0:T(8,128)(2,1)} %constant.82.clone) | copy-start | bytes 442372
  42.4 7.9 %copy-start.3 = (f32[2,144,512]{2,1,0:T(8,128)S(1)}, f32[2,144,512]{2,1,0:T(8,128)}, u32[]{:S(2)}) copy-start(f32[2,144,512]{2,1,0:T(8,128)} %constant.79.clone) | copy-start | bytes 1769476
  42.4 7.9 %copy-start.4 = (f32[2,144,512]{2,1,0:T(8,128)S(1)}, f32[2,144,512]{2,1,0:T(8,128)}, u32[]{:S(2)}) copy-start(f32[2,144,512]{2,1,0:T(8,128)} %constant.80.clone) | copy-start | bytes 1769476
  43.5 6.9 %copy-start.7 = (bf16[288,128]{1,0:T(8,128)(2,1)S(1)}, bf16[288,128]{1,0:T(8,128)(2,1)}, u32[]{:S(2)}) copy-start(bf16[288,128]{1,0:T(8,128)(2,1)} %constant.77.clone) | copy-start | bytes 221188
  43.5 6.9 %copy-start.8 = (bf16[288,128]{1,0:T(8,128)(2,1)S(1)}, bf16[288,128]{1,0:T(8,128)(2,1)}, u32[]{:S(2)}) copy-start(bf16[288,128]{1,0:T(8,128)(2,1)} %constant.78.clone) | copy-start | bytes 221188
  43.8 52.6 %collective-permute-start.1 = (bf16[32,2,512]{0,2,1:T(8,128)(2,1)S(1)}, bf16[32,2,512]{0,2,1:T(8,128)(2,1)S(1)}, u32[]{:S(2)}, u32[]{:S(2)}) collective-permute-start(bf16[32,2,512]{0,2,1:T(8,128)(2,1)S(1)} %get-tuple-element.20), channel_id=1, source_target_pairs={{2,0},{0,2},{6,4},{4,6},{10,8},{8,10},{14,12},{12,14},{18,16},{16,... | collective-permute-start | bytes 196616 | tf_op jit(solution)/shard_map/ppermute | solution.py:222
  48.7 47.7 %collective-permute-start.2 = (bf16[32,2,512]{0,2,1:T(8,128)(2,1)S(1)}, bf16[32,2,512]{0,2,1:T(8,128)(2,1)S(1)}, u32[]{:S(2)}, u32[]{:S(2)}) collective-permute-start(bf16[32,2,512]{0,2,1:T(8,128)(2,1)S(1)} %get-tuple-element.19), channel_id=1, source_target_pairs={{2,1},{0,3},{6,5},{4,7},{10,9},{8,11},{14,13},{12,15},{18,17},{16,... | collective-permute-start | bytes 196616 | tf_op jit(solution)/shard_map/ppermute | solution.py:222
  50.5 53.3 %copy-start = (f32[2,144,512]{2,1,0:T(8,128)}, f32[2,144,512]{2,1,0:T(8,128)S(1)}, u32[]{:S(2)}) copy-start(f32[2,144,512]{2,1,0:T(8,128)S(1)} %broadcast_select_fusion.tw_ref) | copy-start | bytes 1769476
  96.9 56.7 %all-to-all-start = ((bf16[4,16,32,512]{3,2,1,0:T(8,128)(2,1)}), bf16[4,16,32,512]{3,2,1,0:T(8,128)(2,1)}, u32[]{:S(2)}, u32[]{:S(2)}) async-start(bf16[4,16,32,512]{3,2,1,0:T(8,128)(2,1)} %get-tuple-element.11), calls=%async_computation | async-start | bytes 4194304 | tf_op jit(solution)/shard_map/all_to_all | solution.py:237
  123.9 27.4 %collective-permute-start.4 = (bf16[4,16,32,512]{3,2,1,0:T(8,128)(2,1)S(1)}, bf16[4,16,32,512]{3,2,1,0:T(8,128)(2,1)S(1)}, u32[]{:S(2)}, u32[]{:S(2)}) collective-permute-start(bf16[4,16,32,512]{3,2,1,0:T(8,128)(2,1)S(1)} %get-tuple-element.16), channel_id=1, source_target_pairs={{0,4},{4,8},{8,12},{12,16},{16,20},{20,24},{24,28},{1,5},{5,9},{9,... | collective-permute-start | bytes 6291464 | tf_op jit(solution)/shard_map/ppermute | solution.py:239
  153.5 55.2 %all-to-all-start.3 = ((bf16[4,16,32,512]{3,2,1,0:T(8,128)(2,1)}), bf16[4,16,32,512]{3,2,1,0:T(8,128)(2,1)S(1)}, u32[]{:S(2)}, u32[]{:S(2)}) async-start(bf16[4,16,32,512]{3,2,1,0:T(8,128)(2,1)} %add_convert_fusion), calls=%async_computation.3 | async-start | bytes 4194304 | tf_op jit(solution)/shard_map/all_to_all | solution.py:241
  158.6 1.1 copy-start.1
  179.1 27.4 %collective-permute-start.3 = (bf16[4,16,32,512]{3,2,1,0:T(8,128)(2,1)S(1)}, bf16[4,16,32,512]{3,2,1,0:T(8,128)(2,1)S(1)}, u32[]{:S(2)}, u32[]{:S(2)}) collective-permute-start(bf16[4,16,32,512]{3,2,1,0:T(8,128)(2,1)S(1)} %get-tuple-element.13), channel_id=1, source_target_pairs={{0,4},{4,8},{8,12},{12,16},{16,20},{20,24},{24,28},{1,5},{5,9},{9,... | collective-permute-start | bytes 6291464 | tf_op jit(solution)/shard_map/ppermute | solution.py:239
  208.7 53.6 %copy-start.2 = (f32[128]{0:T(128)S(1)}, f32[128]{0:T(128)}, u32[]{:S(2)}) copy-start(f32[128]{0:T(128)} %param.17) | copy-start | bytes 1540
Sparse Core Ops, SparseCore 0:
  25.5 55.6 all-gather.1
